TPU v7x, 32 devices: a whole 2x2x4 slice. The times are simulated.
32 devices in a mesh: dom: 4 (over y, core), space: 8 (over z, x).
Axes of the slice: x: 2, y: 2, z: 4, core: 2. Of those that a mesh axis runs over, the one named last changes fastest.
Arguments:
- orbitals: bfloat16 [4, 2, 32, 16, 8, 128], P('dom', None, 'space'), may hold values from -6 to 6
- initial: bfloat16 [4, 2, 32, 16, 8, 128], P('dom', None, 'space'), may hold values from -4 to 4
- potential: float32 [4, 32, 128], P('dom', 'space'), may hold values from -1 to 1
- external: float32 [4, 32, 128], P('dom', 'space'), may hold values from -1 to 1
- occupation: float32 [128], replicated, may hold values from 0.5 to 2
- coupling: float32 [128, 128], replicated, may hold values from -1.25 to 1.25
- neighbours: int32 [4, 2], replicated, may hold values from 0 to 3, as said below
- offsets: int32 [4, 2], replicated, may hold values from 0 to 12
Outputs:
- evolved: bfloat16 [4, 2, 32, 16, 8, 128], P('dom', None, 'space')
- intersection: float32 [4, 2, 128, 128], P('dom')
- new_potential: float32 [4, 32, 128], P('dom', 'space')
Inputs may be any that keep to these rules, and one draw needn't show every extreme that they name: Following upper neighbours visits all 4 domains in one cycle, and the lower neighbour of a domain's upper neighbour is that domain.
All inputs are finite; a program needn't handle non-finite values.
Results may differ from a plain program's by a relative error of at most 0.007.
Values may be sent and summed in bfloat16 or wider, within the bound.
A program may use at most 64 MiB of HBM per device.

v0:
```python
import jax
import jax.numpy as jnp
from jax import lax
from jax.sharding import PartitionSpec as P

TAYLOR = 4
STEPS = 2
BUF = 4


time_step = 0.4
half_step = 0.2
xc_factor = 0.9847450218426965


def padded_2(value, sides, width):
    for axis, dim in sides:
        devices, length = (lax.axis_size(axis), value.shape[dim])
        up = [(i, (i + 1) % devices) for i in range(devices - 1)]
        down = [(j, i) for i, j in up]
        last = lax.slice_in_dim(value, length - width, length, axis=dim)
        leading = lax.slice_in_dim(value, 0, width, axis=dim)
        before = lax.ppermute(last, axis, up)
        after = lax.ppermute(leading, axis, down)
        value = jnp.concatenate([before, value, after], axis=dim)
    return value


def laplace(source):
    center = source[:, 1:-1]
    total = source[:, 2:] + source[:, :-2] - 6.0 * center
    padded = jnp.pad(center, ((0, 0), (0, 0), (1, 1), (1, 1), (0, 0)))
    total = total + padded[:, :, 2:, 1:-1] + padded[:, :, :-2, 1:-1]
    total = total + padded[:, :, 1:-1, 2:] + padded[:, :, 1:-1, :-2]
    return total


def phase_turn(field, angle):
    cosv = jnp.cos(angle)[..., None]
    sinv = jnp.sin(angle)[..., None]
    return jnp.stack([cosv * field[0] + sinv * field[1], cosv * field[1] - sinv * field[0]])


def kinetic_body(field):
    running = field
    taylor_term = lax.optimization_barrier(field.astype(jnp.bfloat16))
    slab = field.shape[1]
    widened = padded_2(taylor_term, (("space", 1),), TAYLOR)
    first_row = lax.axis_index("space") * slab - TAYLOR
    positions = first_row + jnp.arange(slab + 2 * TAYLOR, dtype=jnp.int32)
    inside = ((positions >= 0) & (positions < slab * lax.axis_size("space"))).astype(jnp.float32)
    source = widened.astype(jnp.float32)
    for order in range(1, TAYLOR + 1):
        curvature = laplace(source)
        width = curvature.shape[1]
        keep = inside[order : order + width].reshape(1, width, 1, 1, 1)
        factor = time_step / (2.0 * order)
        update = jnp.stack([-factor * curvature[1], factor * curvature[0]]) * keep
        running = running + update[:, TAYLOR - order : TAYLOR - order + slab]
        source = lax.optimization_barrier(update.astype(jnp.bfloat16)).astype(jnp.float32)
    return running


def contract(left, right):
    return lax.dot_general(
        left, right, (((0,), (0,)), ((), ())), preferred_element_type=jnp.float32
    )


def select_owner(stacked, owner, domain_ids):
    picked = (domain_ids == owner).reshape((stacked.shape[0],) + (1,) * (stacked.ndim - 1))
    return jnp.sum(jnp.where(picked, stacked, 0.0), axis=0)


def shards(orbitals, initial, potential, external, occupation, coupling, neighbours, offsets):
    field = orbitals[0].astype(jnp.float32)
    start = initial[0]
    slab, rows_y, cols_z, orbit_count = field.shape[1:]
    angle = half_step * potential[0].reshape(slab, rows_y, cols_z)
    cells_total = slab * lax.axis_size("space") * rows_y * cols_z
    flat_start = start.reshape(-1, orbit_count)
    start_real = start[0].reshape(-1, orbit_count)
    start_imag = start[1].reshape(-1, orbit_count)
    shape_one = (slab, rows_y, cols_z, orbit_count)
    intersection = jnp.zeros((2, orbit_count, orbit_count), jnp.float32)
    for section in range(STEPS):
        field = phase_turn(field, angle)
        field = kinetic_body(field)
        field = phase_turn(field, angle)
        rounded = field.astype(jnp.bfloat16)
        over_real = contract(flat_start, rounded.reshape(-1, orbit_count))
        over_imag = contract(start_real, rounded[1].reshape(-1, orbit_count)) - contract(
            start_imag, rounded[0].reshape(-1, orbit_count)
        )
        partial_sum = jnp.stack([over_real, over_imag]) * (1.0 / cells_total)
        intersection = lax.psum(partial_sum, "space")
        mix_real = jnp.dot(coupling, intersection[0], precision=lax.Precision.HIGHEST).astype(
            jnp.bfloat16
        )
        mix_imag = jnp.dot(coupling, intersection[1], precision=lax.Precision.HIGHEST).astype(
            jnp.bfloat16
        )
        corr_real = jnp.dot(start_real, mix_real, preferred_element_type=jnp.float32) - jnp.dot(
            start_imag, mix_imag, preferred_element_type=jnp.float32
        )
        corr_imag = jnp.dot(start_real, mix_imag, preferred_element_type=jnp.float32) + jnp.dot(
            start_imag, mix_real, preferred_element_type=jnp.float32
        )
        field = field + time_step * jnp.stack(
            [corr_imag.reshape(shape_one), -corr_real.reshape(shape_one)]
        )
    density = jnp.sum(field * field * occupation, axis=(0, 4))
    domain_count = neighbours.shape[0]
    domain_ids = jnp.arange(domain_count, dtype=jnp.int32)
    own_index = lax.axis_index("dom")

    def lookup(column, index):
        return jnp.sum(jnp.where(domain_ids == index, column, 0))

    lower_owner = lookup(neighbours[:, 0], own_index)
    upper_owner = lookup(neighbours[:, 1], own_index)
    gathered = lax.all_gather(density.reshape(1, slab, rows_y * cols_z), "dom", axis=0, tiled=True)
    lower_slab = select_owner(gathered, lower_owner, domain_ids).reshape(slab, rows_y, cols_z)
    upper_slab = select_owner(gathered, upper_owner, domain_ids).reshape(slab, rows_y, cols_z)
    lower_brick = lax.dynamic_slice_in_dim(lower_slab, lookup(offsets[:, 0], own_index), BUF, 1)
    upper_brick = lax.dynamic_slice_in_dim(upper_slab, lookup(offsets[:, 1], own_index), BUF, 1)
    planes = jnp.arange(BUF, dtype=jnp.float32)
    weight_low = ((planes + 1.0) / (BUF + 1.0)).reshape(1, BUF, 1)
    weight_high = ((BUF - planes) / (BUF + 1.0)).reshape(1, BUF, 1)
    low = density[:, :BUF] * weight_low + lower_brick * (1.0 - weight_low)
    high = density[:, rows_y - BUF :] * weight_high + upper_brick * (1.0 - weight_high)
    blended = jnp.concatenate([low, density[:, BUF : rows_y - BUF], high], axis=1)
    new_grid = external[0].reshape(slab, rows_y, cols_z) - xc_factor * jnp.cbrt(blended + 1e-06)
    evolved = phase_turn(field, half_step * new_grid).astype(jnp.bfloat16)
    return (evolved[None], intersection[None], new_grid.reshape(1, slab, rows_y * cols_z))


def solution(mesh):
    return jax.shard_map(
        shards,
        mesh=mesh,
        in_specs=(
            P("dom", None, "space", None, None, None),
            P("dom", None, "space", None, None, None),
            P("dom", "space", None),
            P("dom", "space", None),
            P(),
            P(),
            P(),
            P(),
        ),
        out_specs=(
            P("dom", None, "space", None, None, None),
            P("dom", None, None, None),
            P("dom", "space", None),
        ),
        check_vma=False,
    )
```

profile of v0, /device:TPU:0, one launch (start us, length us, event | category | flops | bytes accessed | tf_op | source)
XLA Modules:
  0.0 213.7 jit_solution(12611763736895597904)
XLA Ops:
  7.2 0.7 multiply_cosine_fusion
  8.1 1.0 convert_element_type.118
  9.2 0.2 multiply_add_fusion.3
  9.4 4.9 %collective-permute-start = (bf16[2,4,16,8,128]{4,3,2,1,0:T(8,128)(2,1)S(1)}, bf16[2,4,16,8,128]{4,3,2,1,0:T(8,128)(2,1)S(1)}, u32[]{:S(2)}, u32[]{:S(2)}) collective-permute-start(bf16[2,4,16,8,128]{4,3,2,1,0:T(8,128)(2,1)S(1)} %fusion.55), channel_id=1, source_target_pairs={{0,1},{1,2},{2,3},{3,4},{4,5},{5,6},{6,7},{8,9},{9,10},{10,11},{11... | collective-permute-start | bytes 786440 | tf_op jit(solution)/shard_map/ppermute | solution.py:23
  14.3 1.3 collective-permute-start.1
  15.9 9.5 %collective-permute-done = bf16[2,4,16,8,128]{4,3,2,1,0:T(8,128)(2,1)S(1)} collective-permute-done((bf16[2,4,16,8,128]{4,3,2,1,0:T(8,128)(2,1)S(1)}, bf16[2,4,16,8,128]{4,3,2,1,0:T(8,128)(2,1)S(1)}, u32[]{:S(2)}, u32[]{:S(2)}) %collective-permute-start) | collective-permute-done | bytes 262176 | tf_op jit(solution)/shard_map/ppermute | solution.py:23
  25.7 0.5 fusion.3
  26.3 0.3 fusion.74
  26.9 0.4 fusion.21
  27.4 0.2 fusion.73
  27.8 0.3 fusion.31
  28.8 0.2 fusion.49
  29.0 0.2 multiply_add_fusion.2
  29.3 0.2 fusion.78
  29.5 0.3 convolution_bitcast_fusion.1
  29.8 0.2 fusion.17
  30.0 0.7 maximum_multiply_fusion.10
  30.8 72.0 %all-reduce.11.cloned.1.call-done = f32[2,128,128]{1,2,0:T(8,128)} async-done(((f32[2,128,128]{1,2,0:T(8,128)}), f32[2,128,128]{1,2,0:T(8,128)}) %all-reduce.11.cloned.1.call-update) | async-done | bytes 131088 | tf_op jit(solution)/shard_map/psum | solution.py:96
  102.8 1.1 convolution_convert_fusion.3
  104.1 1.1 convolution_convert_fusion.2
  105.7 0.2 fusion.14
  106.2 0.2 multiply_add_fusion.1
  106.4 2.7 %collective-permute-start.2 = (bf16[2,4,16,8,128]{4,3,2,1,0:T(8,128)(2,1)S(1)}, bf16[2,4,16,8,128]{4,3,2,1,0:T(8,128)(2,1)S(1)}, u32[]{:S(2)}, u32[]{:S(2)}) collective-permute-start(bf16[2,4,16,8,128]{4,3,2,1,0:T(8,128)(2,1)S(1)} %fusion.53), channel_id=1, source_target_pairs={{0,1},{1,2},{2,3},{3,4},{4,5},{5,6},{6,7},{8,9},{9,10},{10,11},{11... | collective-permute-start | bytes 786440 | tf_op jit(solution)/shard_map/ppermute | solution.py:23
  109.1 1.3 collective-permute-start.3
  110.4 0.8 fusion.66
  111.2 0.6 iota_compare_fusion
  111.8 6.7 %collective-permute-done.2 = bf16[2,4,16,8,128]{4,3,2,1,0:T(8,128)(2,1)S(1)} collective-permute-done((bf16[2,4,16,8,128]{4,3,2,1,0:T(8,128)(2,1)S(1)}, bf16[2,4,16,8,128]{4,3,2,1,0:T(8,128)(2,1)S(1)}, u32[]{:S(2)}, u32[]{:S(2)}) %collective-permute-start.2) | collective-permute-done | bytes 262176 | tf_op jit(solution)/shard_map/ppermute | solution.py:23
  118.8 0.5 fusion.7
  119.4 0.3 fusion.71
  120.0 0.4 fusion.25
  120.5 0.2 fusion.70
  120.9 0.3 fusion.35
  121.6 0.2 fusion.45
  121.9 0.2 fusion.47
  122.1 0.2 multiply_add_fusion
  122.4 0.2 fusion.81
  122.6 0.3 convolution_bitcast_fusion
  122.9 0.2 fusion.16
  123.1 0.7 maximum_multiply_fusion.11
  123.8 0.7 iota_compare_fusion.2
  128.5 66.7 %all-reduce.13.cloned.1.call-done = f32[2,128,128]{1,2,0:T(8,128)} async-done(((f32[2,128,128]{1,2,0:T(8,128)}), f32[2,128,128]{1,2,0:T(8,128)}) %all-reduce.13.cloned.1.call-update) | async-done | bytes 131088 | tf_op jit(solution)/shard_map/psum | solution.py:96
  195.3 1.1 convolution_convert_fusion.1
  196.6 1.1 convolution_convert_fusion
  198.8 5.2 %all_gather.3 = f32[4,4,128]{2,1,0:T(4,128)S(1)} all-gather(f32[1,4,128]{2,1,0:T(4,128)S(1)} %reshape.221), channel_id=1, replica_groups=mesh['dom'=4,'space'=8] {'dom'}, dimensions={0}, use_global_device_ids=true | all-gather | bytes 10240 | tf_op jit(solution)/shard_map/all_gather | solution.py:122
  204.6 0.6 sub.133
  205.2 0.8 copy.25
  206.0 0.2 fusion.56
  206.2 0.7 pad_maximum_fusion.4
  (85 shorter events, 6.4 us)
Async XLA Ops:
  7.2 95.6 %copy-start = (f32[128,128]{1,0:T(8,128)S(1)}, f32[128,128]{1,0:T(8,128)}, u32[]{:S(2)}) copy-start(f32[128,128]{1,0:T(8,128)} %param.13) | copy-start | bytes 196612
  7.2 95.6 %all-reduce.11.cloned.1.call-start = ((), (), s32[]{:S(2)}) async-start(), calls=%async_computation | async-start | bytes 262144 | tf_op jit(solution)/shard_map/psum | solution.py:96
  8.1 7.8 %copy-start.1 = (bf16[1,2,4,16,8,128]{5,4,3,2,1,0:T(8,128)(2,1)S(1)}, bf16[1,2,4,16,8,128]{5,4,3,2,1,0:T(8,128)(2,1)}, u32[]{:S(2)}) copy-start(bf16[1,2,4,16,8,128]{5,4,3,2,1,0:T(8,128)(2,1)} %param.9) | copy-start | bytes 786436
  9.4 16.0 %collective-permute-start = (bf16[2,4,16,8,128]{4,3,2,1,0:T(8,128)(2,1)S(1)}, bf16[2,4,16,8,128]{4,3,2,1,0:T(8,128)(2,1)S(1)}, u32[]{:S(2)}, u32[]{:S(2)}) collective-permute-start(bf16[2,4,16,8,128]{4,3,2,1,0:T(8,128)(2,1)S(1)} %fusion.55), channel_id=1, source_target_pairs={{0,1},{1,2},{2,3},{3,4},{4,5},{5,6},{6,7},{8,9},{9,10},{10,11},{11... | collective-permute-start | bytes 786440 | tf_op jit(solution)/shard_map/ppermute | solution.py:23
  14.3 11.2 %collective-permute-start.1 = (bf16[2,4,16,8,128]{4,3,2,1,0:T(8,128)(2,1)S(1)}, bf16[2,4,16,8,128]{4,3,2,1,0:T(8,128)(2,1)S(1)}, u32[]{:S(2)}, u32[]{:S(2)}) collective-permute-start(bf16[2,4,16,8,128]{4,3,2,1,0:T(8,128)(2,1)S(1)} %fusion.55), channel_id=1, source_target_pairs={{1,0},{2,1},{3,2},{4,3},{5,4},{6,5},{7,6},{9,8},{10,9},{11,10},{12... | collective-permute-start | bytes 786440 | tf_op jit(solution)/shard_map/ppermute | solution.py:24
  30.7 164.5 %all-reduce.13.cloned.1.call-start = ((), (), s32[]{:S(2)}) async-start(), calls=%async_computation.1 | async-start | bytes 262144 | tf_op jit(solution)/shard_map/psum | solution.py:96
  106.1 4.3 %copy-start.4 = (s32[4,2]{0,1:T(2,128)S(1)}, s32[4,2]{0,1:T(2,128)}, u32[]{:S(2)}) copy-start(s32[4,2]{0,1:T(2,128)} %param.15) | copy-start | bytes 100
  106.1 4.3 %copy-start.5 = (s32[4,2]{0,1:T(2,128)S(1)}, s32[4,2]{0,1:T(2,128)}, u32[]{:S(2)}) copy-start(s32[4,2]{0,1:T(2,128)} %param.14) | copy-start | bytes 100
  106.4 12.2 %collective-permute-start.2 = (bf16[2,4,16,8,128]{4,3,2,1,0:T(8,128)(2,1)S(1)}, bf16[2,4,16,8,128]{4,3,2,1,0:T(8,128)(2,1)S(1)}, u32[]{:S(2)}, u32[]{:S(2)}) collective-permute-start(bf16[2,4,16,8,128]{4,3,2,1,0:T(8,128)(2,1)S(1)} %fusion.53), channel_id=1, source_target_pairs={{0,1},{1,2},{2,3},{3,4},{4,5},{5,6},{6,7},{8,9},{9,10},{10,11},{11... | collective-permute-start | bytes 786440 | tf_op jit(solution)/shard_map/ppermute | solution.py:23
  109.1 9.5 %collective-permute-start.3 = (bf16[2,4,16,8,128]{4,3,2,1,0:T(8,128)(2,1)S(1)}, bf16[2,4,16,8,128]{4,3,2,1,0:T(8,128)(2,1)S(1)}, u32[]{:S(2)}, u32[]{:S(2)}) collective-permute-start(bf16[2,4,16,8,128]{4,3,2,1,0:T(8,128)(2,1)S(1)} %fusion.53), channel_id=1, source_target_pairs={{1,0},{2,1},{3,2},{4,3},{5,4},{6,5},{7,6},{9,8},{10,9},{11,10},{12... | collective-permute-start | bytes 786440 | tf_op jit(solution)/shard_map/ppermute | solution.py:24
  122.3 4.8 %copy-start.3 = (f32[1,4,128]{2,1,0:T(4,128)S(1)}, f32[1,4,128]{2,1,0:T(4,128)}, u32[]{:S(2)}) copy-start(f32[1,4,128]{2,1,0:T(4,128)} %param.11) | copy-start | bytes 6148
  197.9 0.7 copy-start.6
  198.4 6.8 %copy-start.2 = (f32[2,128,128]{1,2,0:T(8,128)S(1)}, f32[2,128,128]{1,2,0:T(8,128)}, u32[]{:S(2)}) copy-start(f32[2,128,128]{1,2,0:T(8,128)} %all-reduce.13.cloned.1.call-done) | copy-start | bytes 393220
Sparse Core Ops, SparseCore 0:
  30.8 71.9 all-reduce.10
  123.9 71.2 all-reduce.12
where the time goes:
time: 214 us
  waiting for transfers between devices  155 us (72%)
  between operations  18.7 us (9%)
  other arithmetic  14.4 us (7%)
  starting transfers between devices  10.2 us (5%)
  matrix products  7.38 us (3%)
  blocking collectives  5.17 us (2%)
  local copies, waits for them, and re-layouts  2.87 us (1%)
    psum x2, waiting for transfers between devices, shards(): intersection = lax.psum(partial_sum, 'space')  139 us
    ppermute x2, waiting for transfers between devices, padded_2(): before = lax.ppermute(last, axis, up)  16.2 us
    ppermute x2, starting transfers between devices, padded_2(): before = lax.ppermute(last, axis, up)  7.54 us
    all_gather x1, blocking collectives, shards(): lax.all_gather(density.reshape(1, slab, rows_y * cols_z), 'dom', axis=0,...  5.17 us
  transfers between devices with their start and end apart: 6, of which 4 were waited for; matrix products, arithmetic and copies ran while one was open for 1% of the time, Pallas kernels for 0%

commit v1 on v0

v1 whole, which is shorter than its diff:
```python
import functools

import jax
import jax.numpy as jnp
from jax import lax
from jax.experimental import pallas as pl
from jax.experimental.pallas import tpu as pltpu
from jax.sharding import PartitionSpec as P

TAYLOR = 4
STEPS = 2
BUF = 4

time_step = 0.4
half_step = 0.2
xc_factor = 0.9847450218426965

F32 = jnp.float32
BF16 = jnp.bfloat16
HALO = TAYLOR


def body(
    sizes,
    orb,
    ini,
    pot,
    ext,
    occ,
    coup,
    neigh,
    offs,
    evolved_out,
    inter_out,
    pot_out,
    packed,
    other_raw,
    halo_raw,
    other_ini,
    grids,
    source,
    term_a,
    term_b,
    cos_x,
    sin_x,
    field,
    odd,
    rounded,
    turned,
    sums,
    inter,
    dens,
    evolved,
    send_sem,
    recv_sem,
    sum_send,
    sum_recv,
    dens_send,
    dens_recv,
):
    doms, space, slab, rows_y, cols_z, norb = sizes
    cells = rows_y * cols_z
    pairs = space // 2
    half = norb // 2
    main = 2 * slab
    total = main + 2 * HALO
    rows = slab * cells
    edge = HALO * cells
    cells_total = space * rows

    dom = lax.axis_index("dom")
    place = lax.axis_index("space")
    pair = place // 2
    member = place % 2
    partner = (dom, 2 * pair + 1 - member)
    has_lower = pair > 0
    has_upper = pair < pairs - 1
    outward = pair + 2 * member - 1
    has_outward = jnp.logical_and(outward >= 0, outward < pairs)

    def copy(src, dst, ss, rs, device):
        return pltpu.make_async_remote_copy(
            src_ref=src,
            dst_ref=dst,
            send_sem=ss,
            recv_sem=rs,
            device_id=device,
            device_id_type=pl.DeviceIdType.MESH,
        )

    def arrived(dst, rs):
        copy(dst, dst, send_sem.at[0], rs, partner).wait_recv()

    barrier = pltpu.get_barrier_semaphore()

    def greet(device):
        pl.semaphore_signal(barrier, inc=1, device_id=device, device_id_type=pl.DeviceIdType.MESH)

    greet(partner)
    for step in range(1, pairs):
        greet((dom, 2 * ((pair + step) % pairs) + member))
    for step in range(1, doms):
        greet(((dom + step) % doms, 2 * pair))
        greet(((dom + step) % doms, 2 * pair + 1))

    @pl.when(has_outward)
    def _():
        greet((dom, 2 * outward + 1 - member))

    lane = lax.broadcasted_iota(jnp.int32, (cells, norb), 1)
    left = lane < half
    sign = jnp.where(left, -1.0, 1.0).astype(F32)

    def swap(value):
        return pltpu.roll(value, half, 1)

    def at(index, count=1):
        return pl.ds(pl.multiple_of(index * cells, cells), count * cells)

    def pack_plane(j, carry):
        re = orb[0, at(j), :].astype(F32)
        im = orb[1, at(j), :].astype(F32)
        packed[0, at(j), :] = jnp.where(left, re, swap(im)).astype(BF16)
        packed[1, at(j), :] = jnp.where(left, swap(re), im).astype(BF16)
        return carry

    lax.fori_loop(0, slab, pack_plane, 0)
    grids[0, 0:slab, :] = pot[...]
    grids[0, slab:, :] = ext[...]

    pl.semaphore_wait(barrier, pairs + 2 * (doms - 1) + has_outward.astype(jnp.int32))

    grid_swap = copy(grids.at[0], grids.at[1], send_sem.at[0], recv_sem.at[0], partner)
    grid_swap.start()
    role = 1 - member
    grid_edge = [
        copy(
            grids.at[0],
            grids.at[2 + role],
            send_sem.at[1 + k],
            recv_sem.at[1 + role],
            (dom, 2 * outward + k),
        )
        for k in range(2)
    ]
    first = pl.ds(pl.multiple_of(member * (rows - edge), cells), edge)
    raw_edge = [
        copy(
            packed.at[k, first],
            halo_raw.at[role],
            send_sem.at[3 + k],
            recv_sem.at[3 + role],
            (dom, 2 * outward + k),
        )
        for k in range(2)
    ]
    raw_swap = copy(packed.at[1 - member], other_raw, send_sem.at[5], recv_sem.at[5], partner)
    ini_swap = copy(ini, other_ini, send_sem.at[6], recv_sem.at[6], partner)

    @pl.when(has_outward)
    def _():
        for item in grid_edge + raw_edge:
            item.start()

    raw_swap.start()
    ini_swap.start()

    zero_edge = jnp.zeros((edge, norb), BF16)

    @pl.when(jnp.logical_not(has_lower))
    def _():
        grids[2] = jnp.zeros((2 * slab, cells), F32)
        halo_raw[0] = zero_edge
        source[1, 0:edge, :] = zero_edge

    @pl.when(jnp.logical_not(has_upper))
    def _():
        grids[3] = jnp.zeros((2 * slab, cells), F32)
        halo_raw[1] = zero_edge
        source[1, edge + main * cells :, :] = zero_edge

    def spread(angle, first_plane):
        count = angle.shape[0]
        fill = jnp.zeros((norb - 2 * count, cells), F32)
        table = jnp.concatenate([jnp.cos(angle), jnp.sin(angle), fill], axis=0).T
        for j in range(count):
            here = slice((first_plane + j) * cells, (first_plane + j + 1) * cells)
            cos_x[here, :] = jnp.broadcast_to(table[:, j : j + 1], (cells, norb))
            column = table[:, count + j : count + j + 1]
            sin_x[here, :] = jnp.broadcast_to(column, (cells, norb)) * sign

    arrived(grids.at[1], recv_sem.at[0])

    @pl.when(has_lower)
    def _():
        arrived(grids.at[2], recv_sem.at[1])

    @pl.when(has_upper)
    def _():
        arrived(grids.at[3], recv_sem.at[2])

    is_even = member == 0
    mine, theirs = grids[0], grids[1]
    low_grid = jnp.where(is_even, mine, theirs)
    high_grid = jnp.where(is_even, theirs, mine)
    spread(
        half_step
        * jnp.concatenate(
            [grids[2, slab - HALO : slab], low_grid[:slab], high_grid[:slab], grids[3, 0:HALO]],
            axis=0,
        ),
        0,
    )

    def phase(value, j):
        return cos_x[at(j), :] * value - sin_x[at(j), :] * swap(value)

    def begin_own(j, carry):
        plane = HALO + member * slab + j
        value = phase(packed[member, at(j), :].astype(F32), plane)
        field[at(plane - HALO), :] = value
        source[0, at(plane), :] = value.astype(BF16)
        return carry

    def begin_other(j, carry):
        plane = HALO + (1 - member) * slab + j
        value = phase(other_raw[at(j), :].astype(F32), plane)
        field[at(plane - HALO), :] = value
        source[0, at(plane), :] = value.astype(BF16)
        return carry

    def begin_lower(j, carry):
        source[0, at(j), :] = phase(halo_raw[0, at(j), :].astype(F32), j).astype(BF16)
        return carry

    def begin_upper(j, carry):
        plane = HALO + main + j
        source[0, at(plane), :] = phase(halo_raw[1, at(j), :].astype(F32), plane).astype(BF16)
        return carry

    lax.fori_loop(0, slab, begin_own, 0)

    @pl.when(has_lower)
    def _():
        arrived(halo_raw.at[0], recv_sem.at[3])

    @pl.when(has_upper)
    def _():
        arrived(halo_raw.at[1], recv_sem.at[4])

    lax.fori_loop(0, HALO, begin_lower, 0)
    lax.fori_loop(0, HALO, begin_upper, 0)
    arrived(other_raw, recv_sem.at[5])
    lax.fori_loop(0, slab, begin_other, 0)

    z_index = lax.broadcasted_iota(jnp.int32, (rows_y, cols_z, norb), 1)
    z_first = z_index == 0
    z_last = z_index == cols_z - 1
    zero_row = jnp.zeros((1, cols_z, norb), F32)
    lower_keep = has_lower.astype(F32)
    upper_keep = has_upper.astype(F32)

    def curvature(load, j):
        center = load(j).astype(F32).reshape(rows_y, cols_z, norb)
        outer = (load(j - 1).astype(F32) + load(j + 1).astype(F32)).reshape(center.shape)
        value = outer - 6.0 * center
        value = value + jnp.concatenate([center[1:], zero_row], axis=0)
        value = value + jnp.concatenate([zero_row, center[:-1]], axis=0)
        value = value + jnp.where(z_first, 0.0, pltpu.roll(center, 1, 1))
        value = value + jnp.where(z_last, 0.0, pltpu.roll(center, cols_z - 1, 1))
        return value.reshape(cells, norb)

    def kinetic(section):
        def load_source(j):
            return source[section, at(j), :]

        def load_a(j):
            return term_a[at(j), :]

        def load_b(j):
            return term_b[at(j), :]

        loads = [load_source, load_a, load_b, load_a]
        stores = [term_a, term_b, term_a]
        for order in range(1, TAYLOR + 1):
            load = loads[order - 1]
            factor = time_step / (2.0 * order)

            def edge_plane(j, keep, load=load, factor=factor, order=order):
                stores[order - 1][at(j), :] = ((factor * keep) * curvature(load, j)).astype(BF16)

            def lower(j, carry, edge_plane=edge_plane):
                edge_plane(j, lower_keep)
                return carry

            def upper(j, carry, edge_plane=edge_plane):
                edge_plane(j, upper_keep)
                return carry

            def middle(j, carry, load=load, factor=factor, order=order):
                update = factor * curvature(load, j)
                here = at(j - HALO)
                if order < TAYLOR:
                    stores[order - 1][at(j), :] = update.astype(BF16)
                if order == 1:
                    odd[here, :] = update
                elif order == 2:
                    field[here, :] = field[here, :] - update
                elif order == 3:
                    odd[here, :] = odd[here, :] - update
                else:
                    value = field[here, :] + update + sign * swap(odd[here, :])
                    value = phase(value, j)
                    field[here, :] = value
                    near = value.astype(BF16)
                    rounded[here, :] = near
                    turned[here, :] = (-sign * swap(near.astype(F32))).astype(BF16)
                return carry

            if order < TAYLOR:
                lax.fori_loop(order, HALO, lower, 0)
                lax.fori_loop(HALO + main, total - order, upper, 0)
            lax.fori_loop(HALO, HALO + main, middle, 0)

    own_rows = pl.ds(pl.multiple_of(member * rows, cells), rows)
    other_rows = pl.ds(pl.multiple_of((1 - member) * rows, cells), rows)

    def contract(a, b):
        return lax.dot_general(a, b, (((0,), (0,)), ((), ())), preferred_element_type=F32)

    def dot(a, b):
        return jnp.dot(a, b, preferred_element_type=F32)

    edge_sends = []
    sum_sends = []
    result = None
    for section in range(STEPS):
        if section > 0:

            def restart(j, carry):
                value = phase(field[at(j), :], HALO + j)
                field[at(j), :] = value
                source[1, at(HALO + j), :] = value.astype(BF16)
                return carry

            lax.fori_loop(0, main, restart, 0)
            down = copy(
                source.at[1, pl.ds(edge, edge)],
                source.at[1, pl.ds(edge + main * cells, edge)],
                send_sem.at[7],
                recv_sem.at[8],
                (dom, 2 * (pair - 1) + member),
            )
            up = copy(
                source.at[1, pl.ds(main * cells, edge)],
                source.at[1, pl.ds(0, edge)],
                send_sem.at[8],
                recv_sem.at[7],
                (dom, 2 * (pair + 1) + member),
            )

            @pl.when(has_lower)
            def _():
                down.start()

            @pl.when(has_upper)
            def _():
                up.start()

            @pl.when(has_lower)
            def _():
                arrived(source.at[1, pl.ds(0, edge)], recv_sem.at[7])

            @pl.when(has_upper)
            def _():
                arrived(source.at[1, pl.ds(edge + main * cells, edge)], recv_sem.at[8])

            edge_sends = [down, up]
        kinetic(section)
        part = contract(ini[0], rounded[own_rows, :]) + contract(ini[1], turned[own_rows, :])
        if section == 0:
            arrived(other_ini, recv_sem.at[6])
        part = part + contract(other_ini[0], rounded[other_rows, :])
        part = part + contract(other_ini[1], turned[other_rows, :])
        sums[section, pair] = (part * (1.0 / cells_total)).astype(sums.dtype)
        for step in range(1, pairs):
            item = copy(
                sums.at[section, pair],
                sums.at[section, pair],
                sum_send.at[section, step],
                sum_recv.at[section, pair],
                (dom, 2 * ((pair + step) % pairs) + member),
            )
            item.start()
            sum_sends.append(item)
        for step in range(1, pairs):
            slot = (pair + step) % pairs
            arrived(sums.at[section, slot], sum_recv.at[section, slot])
        result = sums[section, 0].astype(F32)
        for slot in range(1, pairs):
            result = result + sums[section, slot].astype(F32)
        if section == STEPS - 1:
            inter[member] = result
            inter_swap = copy(
                inter.at[member], inter.at[member], send_sem.at[9], recv_sem.at[9], partner
            )
            inter_swap.start()
        mix = jnp.dot(
            coup[...], result, precision=lax.Precision.HIGHEST, preferred_element_type=F32
        )
        mix = mix.astype(BF16)
        mix_turned = (-sign[:norb] * swap(mix.astype(F32))).astype(BF16)

        def correct(j, carry, mix=mix, mix_turned=mix_turned):
            own = at(member * slab + j)
            other = at((1 - member) * slab + j)
            gain = dot(ini[0, at(j), :], mix_turned) + dot(ini[1, at(j), :], mix)
            field[own, :] = field[own, :] + time_step * gain
            gain = dot(other_ini[0, at(j), :], mix_turned) + dot(other_ini[1, at(j), :], mix)
            field[other, :] = field[other, :] + time_step * gain
            return carry

        lax.fori_loop(0, slab, correct, 0)

    weight = jnp.broadcast_to(occ[...], (8, norb))
    left_8 = lax.broadcasted_iota(jnp.int32, (8, norb), 1) < half
    keep_own = jnp.logical_xor(left_8, member == 1)
    weight = jnp.where(keep_own, weight, swap(weight))
    own_slot = 2 * dom + member
    lines = []
    for j in range(main):
        value = field[j * cells : (j + 1) * cells, :]
        line = lax.dot_general(
            weight,
            value * value,
            (((1,), (1,)), ((), ())),
            precision=lax.Precision.HIGHEST,
            preferred_element_type=F32,
        )
        lines.append(line[0:1])
    dens[own_slot] = jnp.concatenate(lines, axis=0)
    dens_sends = []
    for step in range(doms):
        for k in range(2):
            if step == 0 and k == 0:
                continue
            item = copy(
                dens.at[own_slot],
                dens.at[own_slot],
                dens_send.at[2 * step + k],
                dens_recv.at[own_slot],
                ((dom + step) % doms, 2 * pair + (member + k) % 2),
            )
            item.start()
            dens_sends.append(item)
    arrived(inter.at[1 - member], recv_sem.at[9])
    inter_out[0] = jnp.where(left[:norb], inter[0], swap(inter[1]))
    inter_out[1] = jnp.where(left[:norb], swap(inter[0]), inter[1])
    for step in range(doms):
        for k in range(2):
            if step == 0 and k == 0:
                continue
            slot = 2 * ((dom + step) % doms) + (member + k) % 2
            arrived(dens.at[slot], dens_recv.at[slot])

    own_density = jnp.zeros((main, cells), F32)
    lower_density = jnp.zeros((main, cells), F32)
    upper_density = jnp.zeros((main, cells), F32)
    lower_owner = neigh[dom, 0]
    upper_owner = neigh[dom, 1]
    lower_offset = offs[dom, 0]
    upper_offset = offs[dom, 1]
    for d in range(doms):
        full = dens[2 * d] + dens[2 * d + 1]
        own_density = jnp.where(dom == d, full, own_density)
        lower_density = jnp.where(lower_owner == d, full, lower_density)
        upper_density = jnp.where(upper_owner == d, full, upper_density)
    low = jnp.zeros((main, cells), F32)
    high = jnp.zeros((main, cells), F32)
    for o in range(rows_y - BUF + 1):
        shift = (cells - o * cols_z) % cells
        moved = pltpu.roll(lower_density, shift, 1) if shift else lower_density
        low = jnp.where(lower_offset == o, moved, low)
        shift = (cells - BUF * cols_z - o * cols_z) % cells
        moved = pltpu.roll(upper_density, shift, 1) if shift else upper_density
        high = jnp.where(upper_offset == o, moved, high)
    y_plane = lax.broadcasted_iota(jnp.int32, (main, cells), 1) // cols_z
    from_top = y_plane - (rows_y - BUF)
    weight_low = (y_plane.astype(F32) + 1.0) / (BUF + 1.0)
    weight_high = (BUF - from_top.astype(F32)) / (BUF + 1.0)
    blended = jnp.where(
        y_plane < BUF,
        own_density * weight_low + low * (1.0 - weight_low),
        jnp.where(
            from_top >= 0, own_density * weight_high + high * (1.0 - weight_high), own_density
        ),
    )
    external = jnp.concatenate([low_grid[slab:], high_grid[slab:]], axis=0)
    root = jnp.exp(jnp.log(blended + 1e-06) * (1.0 / 3.0))
    new_grid = external - xc_factor * root
    pot_out[...] = jnp.where(is_even, new_grid[:slab], new_grid[slab:])
    spread(half_step * new_grid, HALO)

    def finish_other(j, carry):
        plane = (1 - member) * slab + j
        rounded[at(plane), :] = phase(field[at(plane), :], HALO + plane).astype(BF16)
        return carry

    def finish_own(j, carry):
        plane = member * slab + j
        evolved[member, at(j), :] = phase(field[at(plane), :], HALO + plane).astype(BF16)
        return carry

    lax.fori_loop(0, slab, finish_other, 0)
    back = copy(
        rounded.at[other_rows], evolved.at[member], send_sem.at[10], recv_sem.at[10], partner
    )
    back.start()
    lax.fori_loop(0, slab, finish_own, 0)
    arrived(evolved.at[1 - member], recv_sem.at[10])

    def unpack(j, carry):
        zero = evolved[0, at(j), :].astype(F32)
        one = evolved[1, at(j), :].astype(F32)
        evolved_out[0, at(j), :] = jnp.where(left, zero, swap(one)).astype(BF16)
        evolved_out[1, at(j), :] = jnp.where(left, swap(zero), one).astype(BF16)
        return carry

    lax.fori_loop(0, slab, unpack, 0)

    @pl.when(has_outward)
    def _():
        for item in grid_edge + raw_edge:
            item.wait_send()

    @pl.when(has_lower)
    def _():
        edge_sends[0].wait_send()

    @pl.when(has_upper)
    def _():
        edge_sends[1].wait_send()

    for item in [grid_swap, raw_swap, ini_swap, inter_swap, back] + sum_sends + dens_sends:
        item.wait_send()


def shards(orbitals, initial, potential, external, occupation, coupling, neighbours, offsets):
    slab, rows_y, cols_z, norb = orbitals.shape[2:]
    doms = lax.axis_size("dom")
    space = lax.axis_size("space")
    cells = rows_y * cols_z
    rows = slab * cells
    main = 2 * slab
    total = main + 2 * HALO
    pairs = space // 2
    sizes = (doms, space, slab, rows_y, cols_z, norb)
    vmem = pl.BlockSpec(memory_space=pltpu.VMEM)
    smem = pl.BlockSpec(memory_space=pltpu.SMEM)
    dma = pltpu.SemaphoreType.DMA
    evolved, inter, new_grid = pl.pallas_call(
        functools.partial(body, sizes),
        out_shape=(
            jax.ShapeDtypeStruct((2, rows, norb), BF16),
            jax.ShapeDtypeStruct((2, norb, norb), F32),
            jax.ShapeDtypeStruct((slab, cells), F32),
        ),
        in_specs=[vmem] * 6 + [smem] * 2,
        out_specs=(vmem, vmem, vmem),
        scratch_shapes=[
            pltpu.VMEM((2, rows, norb), BF16),
            pltpu.VMEM((rows, norb), BF16),
            pltpu.VMEM((2, HALO * cells, norb), BF16),
            pltpu.VMEM((2, rows, norb), BF16),
            pltpu.VMEM((4, 2 * slab, cells), F32),
            pltpu.VMEM((STEPS, total * cells, norb), BF16),
            pltpu.VMEM((total * cells, norb), BF16),
            pltpu.VMEM((total * cells, norb), BF16),
            pltpu.VMEM((total * cells, norb), F32),
            pltpu.VMEM((total * cells, norb), F32),
            pltpu.VMEM((main * cells, norb), F32),
            pltpu.VMEM((main * cells, norb), F32),
            pltpu.VMEM((main * cells, norb), BF16),
            pltpu.VMEM((main * cells, norb), BF16),
            pltpu.VMEM((STEPS, pairs, norb, norb), BF16),
            pltpu.VMEM((2, norb, norb), F32),
            pltpu.VMEM((2 * doms, main, cells), F32),
            pltpu.VMEM((2, rows, norb), BF16),
            dma((11,)),
            dma((11,)),
            dma((STEPS, pairs)),
            dma((STEPS, pairs)),
            dma((2 * doms,)),
            dma((2 * doms,)),
        ],
        compiler_params=pltpu.CompilerParams(
            collective_id=0, has_side_effects=True, vmem_limit_bytes=32 * 1024 * 1024
        ),
    )(
        orbitals.reshape(2, rows, norb),
        initial.reshape(2, rows, norb),
        potential[0],
        external[0],
        occupation.reshape(1, norb),
        coupling,
        neighbours,
        offsets,
    )
    return (
        evolved.reshape(orbitals.shape),
        inter[None],
        new_grid[None],
    )


def solution(mesh):
    return jax.shard_map(
        shards,
        mesh=mesh,
        in_specs=(
            P("dom", None, "space", None, None, None),
            P("dom", None, "space", None, None, None),
            P("dom", "space", None),
            P("dom", "space", None),
            P(),
            P(),
            P(),
            P(),
        ),
        out_specs=(
            P("dom", None, "space", None, None, None),
            P("dom", None, None, None),
            P("dom", "space", None),
        ),
        check_vma=False,
    )
```

time: 214 us -> 56 us (0.26)
  waiting for transfers between devices: 155 us -> 0 us
  Pallas kernels: 0 us -> 48.3 us
  between operations: 18.7 us -> 0.66 us
  other arithmetic: 14.4 us -> 0 us
  starting transfers between devices: 10.2 us -> 0 us
  matrix products: 7.38 us -> 0 us
  blocking collectives: 5.17 us -> 0 us
  local copies, waits for them, and re-layouts: 2.87 us -> 6.71 us
    psum x2 -> x0, waiting for transfers between devices: 139 us -> none  [shards(): intersection = lax.psum(partial_sum, 'space')]
    pallas_call x0 -> x1, Pallas kernels: none -> 48.3 us  [shards(): pl.pallas_call(functools.partial(body, sizes), out_shape=(jax.ShapeDtypeS...]
    ppermute x4 -> x0, waiting for transfers between devices: 16.3 us -> none  [the longest x2 16.2 us: padded_2(): before = lax.ppermute(last, axis, up)]
    ppermute x4 -> x0, starting transfers between devices: 10.1 us -> none  [the longest x2 7.54 us: padded_2(): before = lax.ppermute(last, axis, up)]
    dot_general x18 -> x0, matrix products: 7.38 us -> none  [the longest x2 2.21 us: shards(): jnp.dot(coupling, intersection[0], precision=lax.Precision.HIGHEST)]
    unnamed x15 -> x21, local copies, waits for them, and re-layouts: 0.8 us -> 6.71 us
    all_gather x1 -> x0, blocking collectives: 5.17 us -> none  [shards(): lax.all_gather(density.reshape(1, slab, rows_y * cols_z), 'dom', axis=0,...]
    add x16 -> x0, other arithmetic: 4.07 us -> none  [the longest x8 2.65 us: laplace(): total = total + padded[:, :, 1:-1, 2:] + padded[:, :, 1:-1, :-2]]
  transfers between devices with their start and end apart: 6 -> 0, of which waited for: 4 -> 0; matrix products, arithmetic and copies ran while one was open for 1% -> 0% of each run, Pallas kernels for 0% -> 0%
where the time goes in v1:
time: 56 us; the launch traced here: 55.7 us
  Pallas kernels  48.3 us (86%)
  local copies, waits for them, and re-layouts  6.71 us (12%)
  between operations  0.66 us (1%)
    pallas_call x1, Pallas kernels, shards(): pl.pallas_call(functools.partial(body, sizes), out_shape=(jax.ShapeDtypeS...  48.3 us
    unnamed x21, local copies, waits for them, and re-layouts  6.71 us

profile of v1, /device:TPU:0, one launch (start us, length us, event | category | flops | bytes accessed | tf_op | source)
XLA Modules:
  0.0 55.7 jit_solution(12200038073395410211)
XLA Ops:
  0.6 0.0 copy-start.6
  0.6 0.7 %copy-done.6 = s32[4,2]{0,1:T(2,128)S(1)} copy-done((s32[4,2]{0,1:T(2,128)S(1)}, s32[4,2]{0,1:T(2,128)}, u32[]{:S(2)}) %copy-start.6) | copy-done | bytes 56
  1.3 0.0 copy-start.7
  1.3 0.0 copy-start.4
  1.3 0.1 copy.11.neigh
  1.4 0.6 %copy-done.7 = s32[4,2]{0,1:T(2,128)S(1)} copy-done((s32[4,2]{0,1:T(2,128)S(1)}, s32[4,2]{0,1:T(2,128)}, u32[]{:S(2)}) %copy-start.7) | copy-done | bytes 56
  2.0 0.0 copy-start.3
  2.0 0.0 copy-start.5
  2.0 0.1 copy.12.offs
  2.1 0.0 copy-done.4
  2.1 0.6 %copy-done.3 = f32[1,4,128]{2,1,0:T(4,128)S(1)} copy-done((f32[1,4,128]{2,1,0:T(4,128)S(1)}, f32[1,4,128]{2,1,0:T(4,128)}, u32[]{:S(2)}) %copy-start.3) | copy-done | bytes 2072
  2.7 0.0 copy-done.5
  2.7 0.0 copy-start
  2.7 0.9 %copy-done = bf16[1,2,4,16,8,128]{5,4,3,2,1,0:T(8,128)(2,1)S(1)} copy-done((bf16[1,2,4,16,8,128]{5,4,3,2,1,0:T(8,128)(2,1)S(1)}, bf16[1,2,4,16,8,128]{5,4,3,2,1,0:T(8,128)(2,1)}, u32[]{:S(2)}) %copy-start) | copy-done | bytes 262168
  3.6 0.0 copy-start.1
  3.6 0.9 %copy-done.1 = bf16[1,2,4,16,8,128]{5,4,3,2,1,0:T(8,128)(2,1)S(1)} copy-done((bf16[1,2,4,16,8,128]{5,4,3,2,1,0:T(8,128)(2,1)S(1)}, bf16[1,2,4,16,8,128]{5,4,3,2,1,0:T(8,128)(2,1)}, u32[]{:S(2)}) %copy-start.1) | copy-done | bytes 262168
  4.6 0.0 copy-start.2
  4.6 0.8 %copy-done.2 = f32[128,128]{1,0:T(8,128)S(1)} copy-done((f32[128,128]{1,0:T(8,128)S(1)}, f32[128,128]{1,0:T(8,128)}, u32[]{:S(2)}) %copy-start.2) | copy-done | bytes 65560
  5.4 48.3 %shard_map.103 = (bf16[2,512,128]{2,1,0:T(8,128)(2,1)S(1)}, f32[2,128,128]{2,1,0:T(8,128)S(1)}, f32[4,128]{1,0:T(4,128)S(1)}) custom-call(bf16[2,512,128]{2,1,0:T(8,128)(2,1)S(1)} %bitcast.8, bf16[2,512,128]{2,1,0:T(8,128)(2,1)S(1)} %bitcast.9, f32[4,128]{1,0:T(4,128)S(1)} %bitcast.12, f32[4,128]{1,0:T(4,128)S(1)} %bitcast.13, f32[1,128]{1,0:T(1,128)S(1)} %bitcast.15, ...), custom_call_target="tpu_custom_call" | custom-call | tf_op jit(solution)/shard_map/pallas_call | solution.py:561
  53.8 0.7 %copy.16 = bf16[1,2,4,16,8,128]{5,4,3,2,1,0:T(8,128)(2,1)} copy(bf16[1,2,4,16,8,128]{5,4,3,2,1,0:T(8,128)(2,1)S(1)} %bitcast.10) | data formatting | bytes 524288
  54.5 0.7 %copy.17 = f32[1,2,128,128]{3,2,1,0:T(8,128)} copy(f32[1,2,128,128]{3,2,1,0:T(8,128)S(1)} %bitcast.11) | data formatting | bytes 262144
  55.1 0.6 %copy.18 = f32[1,4,128]{2,1,0:T(4,128)} copy(f32[1,4,128]{2,1,0:T(4,128)S(1)} %bitcast.14) | data formatting | bytes 4096
Async XLA Ops:
  0.6 0.7 %copy-start.6 = (s32[4,2]{0,1:T(2,128)S(1)}, s32[4,2]{0,1:T(2,128)}, u32[]{:S(2)}) copy-start(s32[4,2]{0,1:T(2,128)} %param.14) | copy-start | bytes 100
  1.3 0.7 %copy-start.7 = (s32[4,2]{0,1:T(2,128)S(1)}, s32[4,2]{0,1:T(2,128)}, u32[]{:S(2)}) copy-start(s32[4,2]{0,1:T(2,128)} %param.15) | copy-start | bytes 100
  1.3 0.8 %copy-start.4 = (f32[1,4,128]{2,1,0:T(4,128)S(1)}, f32[1,4,128]{2,1,0:T(4,128)}, u32[]{:S(2)}) copy-start(f32[1,4,128]{2,1,0:T(4,128)} %param.11) | copy-start | bytes 6148
  2.0 0.7 %copy-start.3 = (f32[1,4,128]{2,1,0:T(4,128)S(1)}, f32[1,4,128]{2,1,0:T(4,128)}, u32[]{:S(2)}) copy-start(f32[1,4,128]{2,1,0:T(4,128)} %param.10) | copy-start | bytes 6148
  2.0 0.7 %copy-start.5 = (f32[128]{0:T(128)S(1)}, f32[128]{0:T(128)}, u32[]{:S(2)}) copy-start(f32[128]{0:T(128)} %param.12) | copy-start | bytes 1540
  2.7 1.0 %copy-start = (bf16[1,2,4,16,8,128]{5,4,3,2,1,0:T(8,128)(2,1)S(1)}, bf16[1,2,4,16,8,128]{5,4,3,2,1,0:T(8,128)(2,1)}, u32[]{:S(2)}) copy-start(bf16[1,2,4,16,8,128]{5,4,3,2,1,0:T(8,128)(2,1)} %param.8) | copy-start | bytes 786436
  3.6 0.9 %copy-start.1 = (bf16[1,2,4,16,8,128]{5,4,3,2,1,0:T(8,128)(2,1)S(1)}, bf16[1,2,4,16,8,128]{5,4,3,2,1,0:T(8,128)(2,1)}, u32[]{:S(2)}) copy-start(bf16[1,2,4,16,8,128]{5,4,3,2,1,0:T(8,128)(2,1)} %param.9) | copy-start | bytes 786436
  4.6 0.8 %copy-start.2 = (f32[128,128]{1,0:T(8,128)S(1)}, f32[128,128]{1,0:T(8,128)}, u32[]{:S(2)}) copy-start(f32[128,128]{1,0:T(8,128)} %coup.1) | copy-start | bytes 196612

commit v2 on v1

v2 whole, which is shorter than its diff:
```python
import functools

import jax
import jax.numpy as jnp
from jax import lax
from jax.experimental import pallas as pl
from jax.experimental.pallas import tpu as pltpu
from jax.sharding import PartitionSpec as P

TAYLOR = 4
STEPS = 2
BUF = 4

time_step = 0.4
half_step = 0.2
xc_factor = 0.9847450218426965

F32 = jnp.float32
BF16 = jnp.bfloat16
HALO = TAYLOR


def body(
    sizes,
    orb_in,
    ini_in,
    pot_in,
    ext_in,
    occ_in,
    coup_in,
    neigh,
    offs,
    evolved_out,
    inter_out,
    pot_out,
    orb,
    ini,
    ext,
    occ,
    coup,
    packed,
    other_raw,
    halo_raw,
    other_ini,
    grids,
    source,
    term_a,
    term_b,
    term_c,
    cos_x,
    sin_x,
    field,
    odd,
    rounded,
    turned,
    sums,
    inter,
    dens,
    returned,
    load_sem,
    send_sem,
    recv_sem,
    sum_send,
    sum_recv,
    dens_send,
    dens_recv,
):
    doms, space, slab, rows_y, cols_z, norb = sizes
    cells = rows_y * cols_z
    pairs = space // 2
    half = norb // 2
    main = 2 * slab
    total = main + 2 * HALO
    rows = slab * cells
    edge = HALO * cells
    cells_total = space * rows

    dom = lax.axis_index("dom")
    place = lax.axis_index("space")
    pair = place // 2
    member = place % 2
    partner = (dom, 2 * pair + 1 - member)
    has_lower = pair > 0
    has_upper = pair < pairs - 1
    outward = pair + 2 * member - 1
    has_outward = jnp.logical_and(outward >= 0, outward < pairs)

    def copy(src, dst, ss, rs, device):
        return pltpu.make_async_remote_copy(
            src_ref=src,
            dst_ref=dst,
            send_sem=ss,
            recv_sem=rs,
            device_id=device,
            device_id_type=pl.DeviceIdType.MESH,
        )

    def arrived(dst, rs):
        copy(dst, dst, send_sem.at[0], rs, partner).wait_recv()

    loads = [
        pltpu.make_async_copy(src, dst, load_sem.at[k])
        for k, (src, dst) in enumerate(
            [
                (orb_in, orb),
                (pot_in, grids.at[0]),
                (ini_in, ini),
                (coup_in, coup),
                (ext_in, ext),
                (occ_in, occ),
            ]
        )
    ]
    for item in loads:
        item.start()
    barrier = pltpu.get_barrier_semaphore()

    def greet(device):
        pl.semaphore_signal(barrier, inc=1, device_id=device, device_id_type=pl.DeviceIdType.MESH)

    greet(partner)
    for step in range(1, pairs):
        greet((dom, 2 * ((pair + step) % pairs) + member))
    for step in range(1, doms):
        greet(((dom + step) % doms, 2 * pair))
        greet(((dom + step) % doms, 2 * pair + 1))

    @pl.when(has_outward)
    def _():
        greet((dom, 2 * outward + 1 - member))

    lane = lax.broadcasted_iota(jnp.int32, (cells, norb), 1)
    left = lane < half
    sign = jnp.where(left, -1.0, 1.0).astype(F32)

    def swap(value):
        return pltpu.roll(value, half, 1)

    def at(index, count=1):
        return pl.ds(pl.multiple_of(index * cells, cells), count * cells)

    def pack_plane(j, carry):
        re = orb[0, at(j), :].astype(F32)
        im = orb[1, at(j), :].astype(F32)
        packed[0, at(j), :] = jnp.where(left, re, swap(im)).astype(BF16)
        packed[1, at(j), :] = jnp.where(left, swap(re), im).astype(BF16)
        return carry

    loads[0].wait()
    lax.fori_loop(0, slab, pack_plane, 0)
    loads[1].wait()

    pl.semaphore_wait(barrier, pairs + 2 * (doms - 1) + has_outward.astype(jnp.int32))

    grid_swap = copy(grids.at[0], grids.at[1], send_sem.at[0], recv_sem.at[0], partner)
    grid_swap.start()
    role = 1 - member
    grid_edge = [
        copy(
            grids.at[0],
            grids.at[2 + role],
            send_sem.at[1 + k],
            recv_sem.at[1 + role],
            (dom, 2 * outward + k),
        )
        for k in range(2)
    ]
    first = pl.ds(pl.multiple_of(member * (rows - edge), cells), edge)
    raw_edge = [
        copy(
            packed.at[k, first],
            halo_raw.at[role],
            send_sem.at[3 + k],
            recv_sem.at[3 + role],
            (dom, 2 * outward + k),
        )
        for k in range(2)
    ]
    raw_swap = copy(packed.at[1 - member], other_raw, send_sem.at[5], recv_sem.at[5], partner)
    ini_swap = copy(ini, other_ini, send_sem.at[6], recv_sem.at[6], partner)

    raw_swap.start()

    @pl.when(has_outward)
    def _():
        for item in grid_edge + raw_edge:
            item.start()


    zero_edge = jnp.zeros((edge, norb), BF16)

    @pl.when(jnp.logical_not(has_lower))
    def _():
        grids[2] = jnp.zeros((slab, cells), F32)
        halo_raw[0] = zero_edge
        source[1, 0:edge, :] = zero_edge

    @pl.when(jnp.logical_not(has_upper))
    def _():
        grids[3] = jnp.zeros((slab, cells), F32)
        halo_raw[1] = zero_edge
        source[1, edge + main * cells :, :] = zero_edge

    def trig_table(angle):
        count = angle.shape[0]
        fill = jnp.zeros((norb - 2 * count, cells), F32)
        return jnp.concatenate([jnp.cos(angle), jnp.sin(angle), fill], axis=0).T

    def spread(angle):
        count = angle.shape[0]
        table = trig_table(angle)
        for j in range(count):
            here = slice(j * cells, (j + 1) * cells)
            cos_x[here, :] = jnp.broadcast_to(table[:, j : j + 1], (cells, norb))
            column = table[:, count + j : count + j + 1]
            sin_x[here, :] = jnp.broadcast_to(column, (cells, norb)) * sign

    arrived(grids.at[1], recv_sem.at[0])

    @pl.when(has_lower)
    def _():
        arrived(grids.at[2], recv_sem.at[1])

    @pl.when(has_upper)
    def _():
        arrived(grids.at[3], recv_sem.at[2])

    is_even = member == 0
    mine, theirs = grids[0], grids[1]
    spread(
        half_step
        * jnp.concatenate(
            [
                grids[2, slab - HALO : slab],
                jnp.where(is_even, mine, theirs),
                jnp.where(is_even, theirs, mine),
                grids[3, 0:HALO],
            ],
            axis=0,
        )
    )

    def phase(value, j):
        return cos_x[at(j), :] * value - sin_x[at(j), :] * swap(value)

    def begin(value, plane):
        value = phase(value.astype(F32), plane)
        field[at(plane), :] = value
        source[0, at(plane), :] = value.astype(BF16)

    def begin_own(j, carry):
        begin(packed[member, at(j), :], HALO + member * slab + j)
        return carry

    def begin_other(j, carry):
        begin(other_raw[at(j), :], HALO + (1 - member) * slab + j)
        return carry

    def begin_edges(j, carry):
        begin(halo_raw[0, at(j), :], j)
        begin(halo_raw[1, at(j), :], HALO + main + j)
        return carry

    lax.fori_loop(0, slab, begin_own, 0)
    arrived(other_raw, recv_sem.at[5])
    lax.fori_loop(0, slab, begin_other, 0)

    z_index = lax.broadcasted_iota(jnp.int32, (rows_y, cols_z, norb), 1)
    z_first = z_index == 0
    z_last = z_index == cols_z - 1
    zero_row = jnp.zeros((1, cols_z, norb), F32)
    lower_keep = has_lower.astype(F32)
    upper_keep = has_upper.astype(F32)

    def curvature(load, j):
        center = load(j).astype(F32).reshape(rows_y, cols_z, norb)
        outer = (load(j - 1).astype(F32) + load(j + 1).astype(F32)).reshape(center.shape)
        value = outer - 6.0 * center
        value = value + jnp.concatenate([center[1:], zero_row], axis=0)
        value = value + jnp.concatenate([zero_row, center[:-1]], axis=0)
        value = value + jnp.where(z_first, 0.0, pltpu.roll(center, 1, 1))
        value = value + jnp.where(z_last, 0.0, pltpu.roll(center, cols_z - 1, 1))
        return value.reshape(cells, norb)

    loads_of = [None, term_a, term_b, term_c]

    def update_of(section, order, j, keep=None):
        factor = time_step / (2.0 * order)
        if keep is not None:
            factor = factor * keep

        def load(plane):
            if order == 1:
                return source[section, at(plane), :]
            return loads_of[order - 1][at(plane), :]

        return factor * curvature(load, j)

    def add_term(order, j, update):
        here = at(j)
        loads_of[order][here, :] = update.astype(BF16)
        if order == 1:
            odd[here, :] = update
        elif order == 2:
            field[here, :] = field[here, :] - update
        else:
            odd[here, :] = odd[here, :] - update

    def add_last(j, update):
        here = at(j)
        value = field[here, :] + update + sign * swap(odd[here, :])
        value = phase(value, j)
        field[here, :] = value
        near = value.astype(BF16)
        rounded[at(j - HALO), :] = near
        turned[at(j - HALO), :] = (-sign * swap(near.astype(F32))).astype(BF16)

    def inner_terms(section):
        for order in range(1, TAYLOR):

            def pair_of_planes(i, carry, order=order):
                j, k = HALO + order + i, HALO + slab + i
                first_update = update_of(section, order, j)
                second_update = update_of(section, order, k)
                add_term(order, j, first_update)
                add_term(order, k, second_update)
                return carry

            if slab > order:
                lax.fori_loop(0, slab - order, pair_of_planes, 0)

    def outer_terms(section):
        for order in range(1, TAYLOR):

            def pair_of_planes(i, carry, order=order):
                j, k = order + i, HALO + main - order + i
                low_keep = jnp.where(j < HALO, lower_keep, 1.0)
                high_keep = jnp.where(k >= HALO + main, upper_keep, 1.0)
                first_update = update_of(section, order, j, low_keep)
                second_update = update_of(section, order, k, high_keep)
                add_term(order, j, first_update)
                add_term(order, k, second_update)
                return carry

            lax.fori_loop(0, HALO, pair_of_planes, 0)

        def last_pair(i, carry):
            j, k = HALO + i, HALO + slab + i
            first_update = update_of(section, TAYLOR, j)
            second_update = update_of(section, TAYLOR, k)
            add_last(j, first_update)
            add_last(k, second_update)
            return carry

        lax.fori_loop(0, slab, last_pair, 0)

    own_rows = pl.ds(pl.multiple_of(member * rows, cells), rows)
    other_rows = pl.ds(pl.multiple_of((1 - member) * rows, cells), rows)

    def contract(a, b):
        return lax.dot_general(a, b, (((0,), (0,)), ((), ())), preferred_element_type=F32)

    def dot(a, b):
        return jnp.dot(a, b, preferred_element_type=F32)

    def correction(section, initials, owner, mixes):
        chunk = 2 if slab % 2 == 0 else 1

        def planes(j, carry):
            from_rows = pl.ds(pl.multiple_of(j * chunk * cells, cells), chunk * cells)
            place_now = owner * slab + j * chunk
            both = jnp.concatenate([initials[0, from_rows, :], initials[1, from_rows, :]], axis=1)
            gain = time_step * dot(both, mixes)
            for k in range(chunk):
                plane = HALO + place_now + k
                value = field[at(plane), :] + gain[k * cells : (k + 1) * cells]
                if section < STEPS - 1:
                    value = phase(value, plane)
                    source[section + 1, at(plane), :] = value.astype(BF16)
                else:
                    rounded[at(plane - HALO), :] = value.astype(BF16)
                field[at(plane), :] = value
            return carry

        lax.fori_loop(0, slab // chunk, planes, 0)

    inward = pair + 1 - 2 * member
    has_inward = jnp.logical_and(inward >= 0, inward < pairs)

    def edge_send(owner, to, k, section):
        here = pl.multiple_of((HALO + owner * (main - HALO)) * cells, cells)
        there = pl.multiple_of((1 - owner) * (HALO + main) * cells, cells)
        return copy(
            source.at[section, pl.ds(here, edge)],
            source.at[section, pl.ds(there, edge)],
            send_sem.at[7 + k],
            recv_sem.at[8 - owner],
            (dom, 2 * to + member),
        )

    edge_out = edge_send(member, outward, 0, 1)
    edge_in = edge_send(1 - member, inward, 1, 1)
    sum_sends = []
    result = None
    for section in range(STEPS):
        inner_terms(section)
        if section == 0:

            @pl.when(has_lower)
            def _():
                arrived(halo_raw.at[0], recv_sem.at[3])

            @pl.when(has_upper)
            def _():
                arrived(halo_raw.at[1], recv_sem.at[4])

            loads[2].wait()
            ini_swap.start()
            lax.fori_loop(0, HALO, begin_edges, 0)
        else:

            @pl.when(has_lower)
            def _():
                arrived(source.at[1, pl.ds(0, edge)], recv_sem.at[7])

            @pl.when(has_upper)
            def _():
                arrived(source.at[1, pl.ds(edge + main * cells, edge)], recv_sem.at[8])

        outer_terms(section)
        part = contract(ini[0], rounded[own_rows, :]) + contract(ini[1], turned[own_rows, :])
        if section == 0:
            arrived(other_ini, recv_sem.at[6])
            loads[3].wait()
        part = part + contract(other_ini[0], rounded[other_rows, :])
        part = part + contract(other_ini[1], turned[other_rows, :])
        sums[section, pair] = (part * (1.0 / cells_total)).astype(sums.dtype)
        for step in range(1, pairs):
            item = copy(
                sums.at[section, pair],
                sums.at[section, pair],
                sum_send.at[section, step],
                sum_recv.at[section, pair],
                (dom, 2 * ((pair + step) % pairs) + member),
            )
            item.start()
            sum_sends.append(item)
        for step in range(1, pairs):
            slot = (pair + step) % pairs
            arrived(sums.at[section, slot], sum_recv.at[section, slot])
        result = sums[section, 0].astype(F32)
        for slot in range(1, pairs):
            result = result + sums[section, slot].astype(F32)
        mix = jnp.dot(
            coup[...], result, precision=lax.Precision.HIGHEST, preferred_element_type=F32
        )
        mix = mix.astype(BF16)
        mix_turned = (-sign[:norb] * swap(mix.astype(F32))).astype(BF16)
        mixes = jnp.concatenate([mix_turned, mix], axis=0)
        correction(section, ini, member, mixes)
        if section < STEPS - 1:

            @pl.when(has_outward)
            def _():
                edge_out.start()

        correction(section, other_ini, 1 - member, mixes)
        if section < STEPS - 1:

            @pl.when(has_inward)
            def _():
                edge_in.start()

    loads[4].wait()
    loads[5].wait()
    weight = jnp.broadcast_to(occ[...], (8, norb))
    left_8 = lax.broadcasted_iota(jnp.int32, (8, norb), 1) < half
    keep_own = jnp.logical_xor(left_8, member == 1)
    weight = jnp.where(keep_own, weight, swap(weight))[0:1]
    own_slot = 2 * dom + member
    lines = []
    for j in range(main):
        value = field[(HALO + j) * cells : (HALO + j + 1) * cells, :]
        lines.append(jnp.sum((value * value * weight).T, axis=0, keepdims=True))
    dens[own_slot] = jnp.concatenate(lines, axis=0)
    dens_sends = []
    for step in range(doms):
        for k in range(2):
            if step == 0 and k == 0:
                continue
            item = copy(
                dens.at[own_slot],
                dens.at[own_slot],
                dens_send.at[2 * step + k],
                dens_recv.at[own_slot],
                ((dom + step) % doms, 2 * pair + (member + k) % 2),
            )
            item.start()
            dens_sends.append(item)
    back = copy(rounded.at[other_rows], returned, send_sem.at[10], recv_sem.at[10], partner)
    back.start()
    inter[member] = result
    inter_swap = copy(
        inter.at[member], inter.at[member], send_sem.at[9], recv_sem.at[9], partner
    )
    inter_swap.start()
    for step in range(doms):
        for k in range(2):
            if step == 0 and k == 0:
                continue
            slot = 2 * ((dom + step) % doms) + (member + k) % 2
            arrived(dens.at[slot], dens_recv.at[slot])

    own_density = jnp.zeros((main, cells), F32)
    lower_density = jnp.zeros((main, cells), F32)
    upper_density = jnp.zeros((main, cells), F32)
    lower_owner = neigh[0, dom]
    upper_owner = neigh[1, dom]
    lower_offset = offs[0, dom]
    upper_offset = offs[1, dom]
    for d in range(doms):
        full = dens[2 * d] + dens[2 * d + 1]
        own_density = jnp.where(dom == d, full, own_density)
        lower_density = jnp.where(lower_owner == d, full, lower_density)
        upper_density = jnp.where(upper_owner == d, full, upper_density)
    low = jnp.zeros((main, cells), F32)
    high = jnp.zeros((main, cells), F32)
    for o in range(rows_y - BUF + 1):
        shift = (cells - o * cols_z) % cells
        moved = pltpu.roll(lower_density, shift, 1) if shift else lower_density
        low = jnp.where(lower_offset == o, moved, low)
        shift = (cells - BUF * cols_z - o * cols_z) % cells
        moved = pltpu.roll(upper_density, shift, 1) if shift else upper_density
        high = jnp.where(upper_offset == o, moved, high)
    y_plane = lax.broadcasted_iota(jnp.int32, (main, cells), 1) // cols_z
    from_top = y_plane - (rows_y - BUF)
    weight_low = (y_plane.astype(F32) + 1.0) / (BUF + 1.0)
    weight_high = (BUF - from_top.astype(F32)) / (BUF + 1.0)
    blended = jnp.where(
        y_plane < BUF,
        own_density * weight_low + low * (1.0 - weight_low),
        jnp.where(
            from_top >= 0, own_density * weight_high + high * (1.0 - weight_high), own_density
        ),
    )
    blended = jnp.where(is_even, blended[:slab], blended[slab:])
    root = jnp.exp(jnp.log(blended + 1e-06) * (1.0 / 3.0))
    new_grid = ext[...] - xc_factor * root
    pot_out[...] = new_grid
    table = trig_table(half_step * new_grid)
    arrived(returned, recv_sem.at[10])

    for j in range(slab):
        here = slice(j * cells, (j + 1) * cells)
        cos_v = table[:, j : j + 1]
        sin_v = table[:, slab + j : slab + j + 1]
        own_half = field[at(HALO + member * slab + j), :]
        other_half = returned[here, :].astype(F32)
        zero = jnp.where(is_even, own_half, other_half)
        one = jnp.where(is_even, other_half, own_half)
        re = jnp.where(left, zero, swap(one))
        im = jnp.where(left, swap(zero), one)
        evolved_out[0, here, :] = (cos_v * re + sin_v * im).astype(BF16)
        evolved_out[1, here, :] = (cos_v * im - sin_v * re).astype(BF16)
    arrived(inter.at[1 - member], recv_sem.at[9])
    inter_out[0] = jnp.where(left[:norb], inter[0], swap(inter[1]))
    inter_out[1] = jnp.where(left[:norb], swap(inter[0]), inter[1])

    @pl.when(has_outward)
    def _():
        for item in grid_edge + raw_edge:
            item.wait_send()

    @pl.when(has_outward)
    def _():
        edge_out.wait_send()

    @pl.when(has_inward)
    def _():
        edge_in.wait_send()

    for item in [grid_swap, raw_swap, ini_swap, inter_swap, back] + sum_sends + dens_sends:
        item.wait_send()


def shards(orbitals, initial, potential, external, occupation, coupling, neighbours, offsets):
    slab, rows_y, cols_z, norb = orbitals.shape[2:]
    doms = lax.axis_size("dom")
    space = lax.axis_size("space")
    cells = rows_y * cols_z
    rows = slab * cells
    main = 2 * slab
    total = main + 2 * HALO
    pairs = space // 2
    sizes = (doms, space, slab, rows_y, cols_z, norb)
    vmem = pl.BlockSpec(memory_space=pltpu.VMEM)
    hbm = pl.BlockSpec(memory_space=pltpu.HBM)
    smem = pl.BlockSpec(memory_space=pltpu.SMEM)
    dma = pltpu.SemaphoreType.DMA
    evolved, inter, new_grid = pl.pallas_call(
        functools.partial(body, sizes),
        out_shape=(
            jax.ShapeDtypeStruct((2, rows, norb), BF16),
            jax.ShapeDtypeStruct((2, norb, norb), F32),
            jax.ShapeDtypeStruct((slab, cells), F32),
        ),
        in_specs=[hbm] * 6 + [smem] * 2,
        out_specs=(vmem, vmem, vmem),
        scratch_shapes=[
            pltpu.VMEM((2, rows, norb), BF16),
            pltpu.VMEM((2, rows, norb), BF16),
            pltpu.VMEM((slab, cells), F32),
            pltpu.VMEM((1, norb), F32),
            pltpu.VMEM((norb, norb), F32),
            pltpu.VMEM((2, rows, norb), BF16),
            pltpu.VMEM((rows, norb), BF16),
            pltpu.VMEM((2, HALO * cells, norb), BF16),
            pltpu.VMEM((2, rows, norb), BF16),
            pltpu.VMEM((4, slab, cells), F32),
            pltpu.VMEM((STEPS, total * cells, norb), BF16),
            pltpu.VMEM((total * cells, norb), BF16),
            pltpu.VMEM((total * cells, norb), BF16),
            pltpu.VMEM((total * cells, norb), BF16),
            pltpu.VMEM((total * cells, norb), F32),
            pltpu.VMEM((total * cells, norb), F32),
            pltpu.VMEM((total * cells, norb), F32),
            pltpu.VMEM((total * cells, norb), F32),
            pltpu.VMEM((main * cells, norb), BF16),
            pltpu.VMEM((main * cells, norb), BF16),
            pltpu.VMEM((STEPS, pairs, norb, norb), BF16),
            pltpu.VMEM((2, norb, norb), F32),
            pltpu.VMEM((2 * doms, main, cells), F32),
            pltpu.VMEM((rows, norb), BF16),
            dma((6,)),
            dma((11,)),
            dma((11,)),
            dma((STEPS, pairs)),
            dma((STEPS, pairs)),
            dma((2 * doms,)),
            dma((2 * doms,)),
        ],
        compiler_params=pltpu.CompilerParams(
            collective_id=0, has_side_effects=True, vmem_limit_bytes=32 * 1024 * 1024
        ),
    )(
        orbitals.reshape(2, rows, norb),
        initial.reshape(2, rows, norb),
        potential[0],
        external[0],
        occupation.reshape(1, norb),
        coupling,
        neighbours.T,
        offsets.T,
    )
    return (
        evolved.reshape(orbitals.shape),
        inter[None],
        new_grid[None],
    )


def solution(mesh):
    return jax.shard_map(
        shards,
        mesh=mesh,
        in_specs=(
            P("dom", None, "space", None, None, None),
            P("dom", None, "space", None, None, None),
            P("dom", "space", None),
            P("dom", "space", None),
            P(),
            P(),
            P(),
            P(),
        ),
        out_specs=(
            P("dom", None, "space", None, None, None),
            P("dom", None, None, None),
            P("dom", "space", None),
        ),
        check_vma=False,
    )
```

time: 56 us -> 50.2 us (0.90)
  Pallas kernels: 48.3 us -> 43.9 us
  local copies, waits for them, and re-layouts: 6.71 us -> 5.36 us
    pallas_call x1, Pallas kernels: 48.3 us -> 43.9 us  [shards(): pl.pallas_call(functools.partial(body, sizes), out_shape=(jax.ShapeDtypeS...]
    unnamed x21 -> x19, local copies, waits for them, and re-layouts: 6.71 us -> 5.36 us
where the time goes in v2:
time: 50.2 us; the launch traced here: 50 us
  Pallas kernels  43.9 us (87%)
  local copies, waits for them, and re-layouts  5.36 us (11%)
  between operations  0.69 us (1%)
    pallas_call x1, Pallas kernels, shards(): pl.pallas_call(functools.partial(body, sizes), out_shape=(jax.ShapeDtypeS...  43.9 us
    unnamed x19, local copies, waits for them, and re-layouts  5.36 us

profile of v2, /device:TPU:0, one launch (start us, length us, event | category | flops | bytes accessed | tf_op | source)
XLA Modules:
  0.0 50.0 jit_solution(910779439016065033)
XLA Ops:
  0.6 0.0 copy-start.6
  0.6 0.0 copy-start.4
  0.7 0.0 copy-start.3
  0.7 0.0 copy-start.5
  0.7 0.0 copy-start.7
  0.7 0.6 %copy-done.6 = s32[4,2]{0,1:T(2,128)S(1)} copy-done((s32[4,2]{0,1:T(2,128)S(1)}, s32[4,2]{0,1:T(2,128)}, u32[]{:S(2)}) %copy-start.6) | copy-done | bytes 56
  1.3 0.0 copy-done.4
  1.3 0.0 copy-done.3
  1.3 0.0 copy-done.5
  1.4 0.0 copy-done.7
  1.4 0.0 copy-start
  1.4 0.9 %copy-done = bf16[1,2,4,16,8,128]{5,4,3,2,1,0:T(8,128)(2,1)S(1)} copy-done((bf16[1,2,4,16,8,128]{5,4,3,2,1,0:T(8,128)(2,1)S(1)}, bf16[1,2,4,16,8,128]{5,4,3,2,1,0:T(8,128)(2,1)}, u32[]{:S(2)}) %copy-start) | copy-done | bytes 262168
  2.3 0.0 copy-start.1
  2.3 0.9 %copy-done.1 = bf16[1,2,4,16,8,128]{5,4,3,2,1,0:T(8,128)(2,1)S(1)} copy-done((bf16[1,2,4,16,8,128]{5,4,3,2,1,0:T(8,128)(2,1)S(1)}, bf16[1,2,4,16,8,128]{5,4,3,2,1,0:T(8,128)(2,1)}, u32[]{:S(2)}) %copy-start.1) | copy-done | bytes 262168
  3.3 0.0 copy-start.2
  3.3 0.8 %copy-done.2 = f32[128,128]{1,0:T(8,128)S(1)} copy-done((f32[128,128]{1,0:T(8,128)S(1)}, f32[128,128]{1,0:T(8,128)}, u32[]{:S(2)}) %copy-start.2) | copy-done | bytes 65560
  4.1 43.9 %shard_map.103 = (bf16[2,512,128]{2,1,0:T(8,128)(2,1)S(1)}, f32[2,128,128]{2,1,0:T(8,128)S(1)}, f32[4,128]{1,0:T(4,128)S(1)}) custom-call(bf16[2,512,128]{2,1,0:T(8,128)(2,1)S(1)} %bitcast.10, bf16[2,512,128]{2,1,0:T(8,128)(2,1)S(1)} %bitcast.11, f32[4,128]{1,0:T(4,128)S(1)} %bitcast.14, f32[4,128]{1,0:T(4,128)S(1)} %bitcast.15, f32[1,128]{1,0:T(1,128)S(1)} %bitcast.19, ...), custom_call_target="tpu_custom_call" | custom-call | tf_op jit(solution)/shard_map/pallas_call | solution.py:600
  48.0 0.7 %copy.14 = bf16[1,2,4,16,8,128]{5,4,3,2,1,0:T(8,128)(2,1)} copy(bf16[1,2,4,16,8,128]{5,4,3,2,1,0:T(8,128)(2,1)S(1)} %bitcast.12) | data formatting | bytes 524288
  48.7 0.7 %copy.15 = f32[1,2,128,128]{3,2,1,0:T(8,128)} copy(f32[1,2,128,128]{3,2,1,0:T(8,128)S(1)} %bitcast.13) | data formatting | bytes 262144
  49.4 0.6 %copy.16 = f32[1,4,128]{2,1,0:T(4,128)} copy(f32[1,4,128]{2,1,0:T(4,128)S(1)} %bitcast.16) | data formatting | bytes 4096
Async XLA Ops:
  0.6 0.7 %copy-start.6 = (s32[4,2]{0,1:T(2,128)S(1)}, s32[4,2]{0,1:T(2,128)}, u32[]{:S(2)}) copy-start(s32[4,2]{0,1:T(2,128)} %param.15) | copy-start | bytes 100
  0.6 0.7 %copy-start.4 = (f32[1,4,128]{2,1,0:T(4,128)S(1)}, f32[1,4,128]{2,1,0:T(4,128)}, u32[]{:S(2)}) copy-start(f32[1,4,128]{2,1,0:T(4,128)} %param.11) | copy-start | bytes 6148
  0.7 0.7 %copy-start.3 = (f32[1,4,128]{2,1,0:T(4,128)S(1)}, f32[1,4,128]{2,1,0:T(4,128)}, u32[]{:S(2)}) copy-start(f32[1,4,128]{2,1,0:T(4,128)} %param.10) | copy-start | bytes 6148
  0.7 0.7 %copy-start.5 = (s32[4,2]{0,1:T(2,128)S(1)}, s32[4,2]{0,1:T(2,128)}, u32[]{:S(2)}) copy-start(s32[4,2]{0,1:T(2,128)} %param.14) | copy-start | bytes 100
  0.7 0.7 %copy-start.7 = (f32[128]{0:T(128)S(1)}, f32[128]{0:T(128)}, u32[]{:S(2)}) copy-start(f32[128]{0:T(128)} %param.12) | copy-start | bytes 1540
  1.4 1.0 %copy-start = (bf16[1,2,4,16,8,128]{5,4,3,2,1,0:T(8,128)(2,1)S(1)}, bf16[1,2,4,16,8,128]{5,4,3,2,1,0:T(8,128)(2,1)}, u32[]{:S(2)}) copy-start(bf16[1,2,4,16,8,128]{5,4,3,2,1,0:T(8,128)(2,1)} %param.8) | copy-start | bytes 786436
  2.3 0.9 %copy-start.1 = (bf16[1,2,4,16,8,128]{5,4,3,2,1,0:T(8,128)(2,1)S(1)}, bf16[1,2,4,16,8,128]{5,4,3,2,1,0:T(8,128)(2,1)}, u32[]{:S(2)}) copy-start(bf16[1,2,4,16,8,128]{5,4,3,2,1,0:T(8,128)(2,1)} %param.9) | copy-start | bytes 786436
  3.3 0.8 %copy-start.2 = (f32[128,128]{1,0:T(8,128)S(1)}, f32[128,128]{1,0:T(8,128)}, u32[]{:S(2)}) copy-start(f32[128,128]{1,0:T(8,128)} %coup_in.1) | copy-start | bytes 196612

commit v3 on v2

--- a/solution.py
+++ b/solution.py
@@ -64,6 +64,10 @@
     sum_recv,
     dens_send,
     dens_recv,
+    swap_send,
+    swap_recv,
+    edge_send_sem,
+    edge_recv_sem,
 ):
     doms, space, slab, rows_y, cols_z, norb = sizes
     cells = rows_y * cols_z
@@ -84,6 +88,9 @@
     has_upper = pair < pairs - 1
     outward = pair + 2 * member - 1
     has_outward = jnp.logical_and(outward >= 0, outward < pairs)
+    inward = pair + 1 - 2 * member
+    has_inward = jnp.logical_and(inward >= 0, inward < pairs)
+    chunks = 2 if slab == HALO and slab % 2 == 0 else 1
 
     def copy(src, dst, ss, rs, device):
         return pltpu.make_async_remote_copy(
@@ -125,10 +132,6 @@
         greet(((dom + step) % doms, 2 * pair))
         greet(((dom + step) % doms, 2 * pair + 1))
 
-    @pl.when(has_outward)
-    def _():
-        greet((dom, 2 * outward + 1 - member))
-
     lane = lax.broadcasted_iota(jnp.int32, (cells, norb), 1)
     left = lane < half
     sign = jnp.where(left, -1.0, 1.0).astype(F32)
@@ -150,42 +153,68 @@
     lax.fori_loop(0, slab, pack_plane, 0)
     loads[1].wait()
 
-    pl.semaphore_wait(barrier, pairs + 2 * (doms - 1) + has_outward.astype(jnp.int32))
+    pl.semaphore_wait(barrier, pairs + 2 * (doms - 1))
 
     grid_swap = copy(grids.at[0], grids.at[1], send_sem.at[0], recv_sem.at[0], partner)
     grid_swap.start()
     role = 1 - member
-    grid_edge = [
+    onward = (dom, 2 * outward + member)
+    back_in = (dom, 2 * inward + member)
+    grid_edge = copy(
+        grids.at[0], grids.at[2 + role], send_sem.at[1], recv_sem.at[1 + role], onward
+    )
+    grid_forward = copy(
+        grids.at[1], grids.at[2 + member], send_sem.at[2], recv_sem.at[1 + member], back_in
+    )
+    swap_rows = rows // chunks
+    edge_rows = edge // chunks
+
+    def span(c, length):
+        return pl.ds(c * length, length)
+
+    def edge_span(owner, c):
+        start = owner * (rows - edge) + c * edge_rows
+        return pl.ds(pl.multiple_of(start, cells), edge_rows)
+
+    raw_swap = [
         copy(
-            grids.at[0],
-            grids.at[2 + role],
-            send_sem.at[1 + k],
-            recv_sem.at[1 + role],
-            (dom, 2 * outward + k),
+            packed.at[1 - member, span(c, swap_rows)],
+            other_raw.at[span(c, swap_rows)],
+            swap_send.at[c],
+            swap_recv.at[c],
+            partner,
         )
-        for k in range(2)
+        for c in range(chunks)
     ]
-    first = pl.ds(pl.multiple_of(member * (rows - edge), cells), edge)
     raw_edge = [
         copy(
-            packed.at[k, first],
-            halo_raw.at[role],
-            send_sem.at[3 + k],
-            recv_sem.at[3 + role],
-            (dom, 2 * outward + k),
+            packed.at[member, edge_span(member, c)],
+            halo_raw.at[role, span(c, edge_rows)],
+            edge_send_sem.at[0, c],
+            edge_recv_sem.at[role, c],
+            onward,
         )
-        for k in range(2)
+        for c in range(chunks)
     ]
-    raw_swap = copy(packed.at[1 - member], other_raw, send_sem.at[5], recv_sem.at[5], partner)
+    raw_forward = [
+        copy(
+            other_raw.at[edge_span(1 - member, c)],
+            halo_raw.at[member, span(c, edge_rows)],
+            edge_send_sem.at[1, c],
+            edge_recv_sem.at[member, c],
+            back_in,
+        )
+        for c in range(chunks)
+    ]
     ini_swap = copy(ini, other_ini, send_sem.at[6], recv_sem.at[6], partner)
-
-    raw_swap.start()
+    for item in raw_swap:
+        item.start()
 
     @pl.when(has_outward)
     def _():
-        for item in grid_edge + raw_edge:
+        grid_edge.start()
+        for item in raw_edge:
             item.start()
-
 
     zero_edge = jnp.zeros((edge, norb), BF16)
 
@@ -206,39 +235,25 @@
         fill = jnp.zeros((norb - 2 * count, cells), F32)
         return jnp.concatenate([jnp.cos(angle), jnp.sin(angle), fill], axis=0).T
 
-    def spread(angle):
+    def spread(angle, planes):
         count = angle.shape[0]
         table = trig_table(angle)
-        for j in range(count):
-            here = slice(j * cells, (j + 1) * cells)
+        for j, plane in enumerate(planes):
+            here = slice(plane * cells, (plane + 1) * cells)
             cos_x[here, :] = jnp.broadcast_to(table[:, j : j + 1], (cells, norb))
             column = table[:, count + j : count + j + 1]
             sin_x[here, :] = jnp.broadcast_to(column, (cells, norb)) * sign
 
     arrived(grids.at[1], recv_sem.at[0])
 
-    @pl.when(has_lower)
+    @pl.when(has_inward)
     def _():
-        arrived(grids.at[2], recv_sem.at[1])
-
-    @pl.when(has_upper)
-    def _():
-        arrived(grids.at[3], recv_sem.at[2])
+        grid_forward.start()
 
     is_even = member == 0
     mine, theirs = grids[0], grids[1]
-    spread(
-        half_step
-        * jnp.concatenate(
-            [
-                grids[2, slab - HALO : slab],
-                jnp.where(is_even, mine, theirs),
-                jnp.where(is_even, theirs, mine),
-                grids[3, 0:HALO],
-            ],
-            axis=0,
-        )
-    )
+    both_grids = [jnp.where(is_even, mine, theirs), jnp.where(is_even, theirs, mine)]
+    spread(half_step * jnp.concatenate(both_grids, axis=0), range(HALO, HALO + main))
 
     def phase(value, j):
         return cos_x[at(j), :] * value - sin_x[at(j), :] * swap(value)
@@ -262,8 +277,17 @@
         return carry
 
     lax.fori_loop(0, slab, begin_own, 0)
-    arrived(other_raw, recv_sem.at[5])
-    lax.fori_loop(0, slab, begin_other, 0)
+    for c in range(chunks):
+        arrived(other_raw.at[span(c, swap_rows)], swap_recv.at[c])
+
+        @pl.when(has_inward)
+        def _():
+            raw_forward[c].start()
+
+        if c == 0:
+            loads[2].wait()
+            ini_swap.start()
+        lax.fori_loop(c * (slab // chunks), (c + 1) * (slab // chunks), begin_other, 0)
 
     z_index = lax.broadcasted_iota(jnp.int32, (rows_y, cols_z, norb), 1)
     z_first = z_index == 0
@@ -384,9 +408,6 @@
 
         lax.fori_loop(0, slab // chunk, planes, 0)
 
-    inward = pair + 1 - 2 * member
-    has_inward = jnp.logical_and(inward >= 0, inward < pairs)
-
     def edge_send(owner, to, k, section):
         here = pl.multiple_of((HALO + owner * (main - HALO)) * cells, cells)
         there = pl.multiple_of((1 - owner) * (HALO + main) * cells, cells)
@@ -408,14 +429,25 @@
 
             @pl.when(has_lower)
             def _():
-                arrived(halo_raw.at[0], recv_sem.at[3])
+                arrived(grids.at[2], recv_sem.at[1])
 
             @pl.when(has_upper)
             def _():
-                arrived(halo_raw.at[1], recv_sem.at[4])
-
-            loads[2].wait()
-            ini_swap.start()
+                arrived(grids.at[3], recv_sem.at[2])
+
+            ends = jnp.concatenate([grids[2, slab - HALO : slab], grids[3, 0:HALO]], axis=0)
+            spread(half_step * ends, [*range(HALO), *range(HALO + main, total)])
+
+            @pl.when(has_lower)
+            def _():
+                for c in range(chunks):
+                    arrived(halo_raw.at[0, span(c, edge_rows)], edge_recv_sem.at[0, c])
+
+            @pl.when(has_upper)
+            def _():
+                for c in range(chunks):
+                    arrived(halo_raw.at[1, span(c, edge_rows)], edge_recv_sem.at[1, c])
+
             lax.fori_loop(0, HALO, begin_edges, 0)
         else:
 
@@ -568,7 +600,7 @@
 
     @pl.when(has_outward)
     def _():
-        for item in grid_edge + raw_edge:
+        for item in [grid_edge] + raw_edge:
             item.wait_send()
 
     @pl.when(has_outward)
@@ -578,8 +610,10 @@
     @pl.when(has_inward)
     def _():
         edge_in.wait_send()
-
-    for item in [grid_swap, raw_swap, ini_swap, inter_swap, back] + sum_sends + dens_sends:
+        for item in [grid_forward] + raw_forward:
+            item.wait_send()
+
+    for item in [grid_swap, ini_swap, inter_swap, back] + raw_swap + sum_sends + dens_sends:
         item.wait_send()
 
 
@@ -638,9 +672,13 @@
             dma((STEPS, pairs)),
             dma((2 * doms,)),
             dma((2 * doms,)),
+            dma((2,)),
+            dma((2,)),
+            dma((2, 2)),
+            dma((2, 2)),
         ],
         compiler_params=pltpu.CompilerParams(
-            collective_id=0, has_side_effects=True, vmem_limit_bytes=32 * 1024 * 1024
+            collective_id=0, has_side_effects=True, vmem_limit_bytes=60 * 1024 * 1024
         ),
     )(
         orbitals.reshape(2, rows, norb),

time: 50.2 us -> 43.9 us (0.87)
  Pallas kernels: 43.9 us -> 40.1 us
  local copies, waits for them, and re-layouts: 5.36 us -> 2.95 us
    pallas_call x1, Pallas kernels: 43.9 us -> 40.1 us  [shards(): pl.pallas_call(functools.partial(body, sizes), out_shape=(jax.ShapeDtypeS...]
    unnamed x19 -> x7, local copies, waits for them, and re-layouts: 5.36 us -> 2.95 us
where the time goes in v3:
time: 43.9 us; the launch traced here: 43.7 us
  Pallas kernels  40.1 us (91%)
  local copies, waits for them, and re-layouts  2.95 us (7%)
  between operations  0.65 us (1%)
    pallas_call x1, Pallas kernels, shards(): pl.pallas_call(functools.partial(body, sizes), out_shape=(jax.ShapeDtypeS...  40.1 us
    unnamed x7, local copies, waits for them, and re-layouts  2.95 us

profile of v3, /device:TPU:0, one launch (start us, length us, event | category | flops | bytes accessed | tf_op | source)
XLA Modules:
  0.0 43.7 jit_solution(15675405439923636082)
XLA Ops:
  0.6 40.1 %shard_map.103 = (bf16[2,512,128]{2,1,0:T(8,128)(2,1)}, f32[2,128,128]{2,1,0:T(8,128)}, f32[4,128]{1,0:T(4,128)}) custom-call(bf16[2,512,128]{2,1,0:T(8,128)(2,1)} %bitcast.10, bf16[2,512,128]{2,1,0:T(8,128)(2,1)} %bitcast.11, f32[4,128]{1,0:T(4,128)} %bitcast.14, f32[4,128]{1,0:T(4,128)} %bitcast.15, f32[1,128]{1,0:T(1,128)} %bitcast.19, ...), custom_call_target="tpu_custom_call" | custom-call | tf_op jit(solution)/shard_map/pallas_call | solution.py:634
  40.7 0.0 copy-start
  40.7 1.7 %copy.14 = bf16[1,2,4,16,8,128]{5,4,3,2,1,0:T(8,128)(2,1)} copy(bf16[1,2,4,16,8,128]{5,4,3,2,1,0:T(8,128)(2,1)} %bitcast.12) | data formatting | bytes 524288
  42.5 0.0 copy-done
  42.5 0.0 copy-start.1
  42.5 0.7 %copy.15 = f32[1,2,128,128]{3,2,1,0:T(8,128)} copy(f32[1,2,128,128]{3,2,1,0:T(8,128)S(1)} %bitcast.13) | data formatting | bytes 262144
  43.1 0.0 copy-done.1
  43.1 0.6 %copy.16 = f32[1,4,128]{2,1,0:T(4,128)} copy(f32[1,4,128]{2,1,0:T(4,128)S(1)} %bitcast.16) | data formatting | bytes 4096
Async XLA Ops:
  40.7 1.7 %copy-start = (f32[2,128,128]{2,1,0:T(8,128)S(1)}, f32[2,128,128]{2,1,0:T(8,128)}, u32[]{:S(2)}) copy-start(f32[2,128,128]{2,1,0:T(8,128)} %get-tuple-element.7) | copy-start | bytes 393220
  42.5 0.7 %copy-start.1 = (f32[4,128]{1,0:T(4,128)S(1)}, f32[4,128]{1,0:T(4,128)}, u32[]{:S(2)}) copy-start(f32[4,128]{1,0:T(4,128)} %get-tuple-element.8) | copy-start | bytes 6148

commit v4 on v3

--- a/solution.py
+++ b/solution.py
@@ -68,6 +68,10 @@
     swap_recv,
     edge_send_sem,
     edge_recv_sem,
+    step_send,
+    step_recv,
+    own_turned,
+    other_turned,
 ):
     doms, space, slab, rows_y, cols_z, norb = sizes
     cells = rows_y * cols_z
@@ -90,7 +94,6 @@
     has_outward = jnp.logical_and(outward >= 0, outward < pairs)
     inward = pair + 1 - 2 * member
     has_inward = jnp.logical_and(inward >= 0, inward < pairs)
-    chunks = 2 if slab == HALO and slab % 2 == 0 else 1
 
     def copy(src, dst, ss, rs, device):
         return pltpu.make_async_remote_copy(
@@ -166,45 +169,42 @@
     grid_forward = copy(
         grids.at[1], grids.at[2 + member], send_sem.at[2], recv_sem.at[1 + member], back_in
     )
-    swap_rows = rows // chunks
-    edge_rows = edge // chunks
-
-    def span(c, length):
-        return pl.ds(c * length, length)
-
-    def edge_span(owner, c):
-        start = owner * (rows - edge) + c * edge_rows
-        return pl.ds(pl.multiple_of(start, cells), edge_rows)
+
+    def ranked(owner, i):
+        return i + owner * (slab - 1 - 2 * i)
+
+    def in_halo(owner, i):
+        return i + owner * (HALO - 1 - 2 * i)
 
     raw_swap = [
         copy(
-            packed.at[1 - member, span(c, swap_rows)],
-            other_raw.at[span(c, swap_rows)],
-            swap_send.at[c],
-            swap_recv.at[c],
+            packed.at[1 - member, at(ranked(member, i))],
+            other_raw.at[at(ranked(member, i))],
+            swap_send.at[i],
+            swap_recv.at[i],
             partner,
         )
-        for c in range(chunks)
+        for i in range(slab)
     ]
     raw_edge = [
         copy(
-            packed.at[member, edge_span(member, c)],
-            halo_raw.at[role, span(c, edge_rows)],
-            edge_send_sem.at[0, c],
-            edge_recv_sem.at[role, c],
+            packed.at[member, at(ranked(member, i))],
+            halo_raw.at[role, at(in_halo(member, i))],
+            edge_send_sem.at[0, i],
+            edge_recv_sem.at[role, i],
             onward,
         )
-        for c in range(chunks)
+        for i in range(HALO)
     ]
     raw_forward = [
         copy(
-            other_raw.at[edge_span(1 - member, c)],
-            halo_raw.at[member, span(c, edge_rows)],
-            edge_send_sem.at[1, c],
-            edge_recv_sem.at[member, c],
+            other_raw.at[at(ranked(1 - member, i))],
+            halo_raw.at[member, at(in_halo(1 - member, i))],
+            edge_send_sem.at[1, i],
+            edge_recv_sem.at[member, i],
             back_in,
         )
-        for c in range(chunks)
+        for i in range(HALO)
     ]
     ini_swap = copy(ini, other_ini, send_sem.at[6], recv_sem.at[6], partner)
     for item in raw_swap:
@@ -267,27 +267,23 @@
         begin(packed[member, at(j), :], HALO + member * slab + j)
         return carry
 
-    def begin_other(j, carry):
-        begin(other_raw[at(j), :], HALO + (1 - member) * slab + j)
-        return carry
-
-    def begin_edges(j, carry):
-        begin(halo_raw[0, at(j), :], j)
-        begin(halo_raw[1, at(j), :], HALO + main + j)
-        return carry
-
     lax.fori_loop(0, slab, begin_own, 0)
-    for c in range(chunks):
-        arrived(other_raw.at[span(c, swap_rows)], swap_recv.at[c])
-
-        @pl.when(has_inward)
-        def _():
-            raw_forward[c].start()
-
-        if c == 0:
-            loads[2].wait()
+    loads[2].wait()
+    for half_index in range(2):
+        own_turned[half_index] = ini[half_index].T
+    for i in range(slab):
+        plane = ranked(1 - member, i)
+        arrived(other_raw.at[at(plane)], swap_recv.at[i])
+        if i < HALO:
+
+            @pl.when(has_inward)
+            def _():
+                raw_forward[i].start()
+
+        if i == slab // 2:
             ini_swap.start()
-        lax.fori_loop(c * (slab // chunks), (c + 1) * (slab // chunks), begin_other, 0)
+
+        begin(other_raw[at(plane), :], HALO + (1 - member) * slab + plane)
 
     z_index = lax.broadcasted_iota(jnp.int32, (rows_y, cols_z, norb), 1)
     z_first = z_index == 0
@@ -340,49 +336,63 @@
         turned[at(j - HALO), :] = (-sign * swap(near.astype(F32))).astype(BF16)
 
     def inner_terms(section):
-        for order in range(1, TAYLOR):
+        for order in range(1, TAYLOR + 1):
 
             def pair_of_planes(i, carry, order=order):
                 j, k = HALO + order + i, HALO + slab + i
                 first_update = update_of(section, order, j)
                 second_update = update_of(section, order, k)
-                add_term(order, j, first_update)
-                add_term(order, k, second_update)
+                add = add_term if order < TAYLOR else lambda _, *rest: add_last(*rest)
+                add(order, j, first_update)
+                add(order, k, second_update)
                 return carry
 
             if slab > order:
                 lax.fori_loop(0, slab - order, pair_of_planes, 0)
 
     def outer_terms(section):
-        for order in range(1, TAYLOR):
-
-            def pair_of_planes(i, carry, order=order):
-                j, k = order + i, HALO + main - order + i
+        def diagonal(i, carry):
+            low, high = HALO - 1 - i, HALO + main + i
+            if section == 0:
+
+                @pl.when(has_lower)
+                def _():
+                    arrived(halo_raw.at[0, at(low)], edge_recv_sem.at[0, i])
+
+                @pl.when(has_upper)
+                def _():
+                    arrived(halo_raw.at[1, at(i)], edge_recv_sem.at[1, i])
+
+                begin(halo_raw[0, at(low), :], low)
+                begin(halo_raw[1, at(i), :], high)
+            else:
+
+                @pl.when(has_lower)
+                def _():
+                    arrived(source.at[section, at(low)], step_recv.at[0, i])
+
+                @pl.when(has_upper)
+                def _():
+                    arrived(source.at[section, at(high)], step_recv.at[1, i])
+
+            for order in range(1, TAYLOR + 1):
+                j, k = low + order, high - order
                 low_keep = jnp.where(j < HALO, lower_keep, 1.0)
                 high_keep = jnp.where(k >= HALO + main, upper_keep, 1.0)
                 first_update = update_of(section, order, j, low_keep)
                 second_update = update_of(section, order, k, high_keep)
-                add_term(order, j, first_update)
-                add_term(order, k, second_update)
-                return carry
-
-            lax.fori_loop(0, HALO, pair_of_planes, 0)
-
-        def last_pair(i, carry):
-            j, k = HALO + i, HALO + slab + i
-            first_update = update_of(section, TAYLOR, j)
-            second_update = update_of(section, TAYLOR, k)
-            add_last(j, first_update)
-            add_last(k, second_update)
+                add = add_term if order < TAYLOR else lambda _, *rest: add_last(*rest)
+                add(order, j, first_update)
+                add(order, k, second_update)
             return carry
 
-        lax.fori_loop(0, slab, last_pair, 0)
+        lax.fori_loop(0, HALO, diagonal, 0)
 
     own_rows = pl.ds(pl.multiple_of(member * rows, cells), rows)
     other_rows = pl.ds(pl.multiple_of((1 - member) * rows, cells), rows)
 
     def contract(a, b):
-        return lax.dot_general(a, b, (((0,), (0,)), ((), ())), preferred_element_type=F32)
+        return jnp.dot(a, b, preferred_element_type=F32)
 
     def dot(a, b):
         return jnp.dot(a, b, preferred_element_type=F32)
@@ -408,19 +418,20 @@
 
         lax.fori_loop(0, slab // chunk, planes, 0)
 
-    def edge_send(owner, to, k, section):
-        here = pl.multiple_of((HALO + owner * (main - HALO)) * cells, cells)
-        there = pl.multiple_of((1 - owner) * (HALO + main) * cells, cells)
-        return copy(
-            source.at[section, pl.ds(here, edge)],
-            source.at[section, pl.ds(there, edge)],
-            send_sem.at[7 + k],
-            recv_sem.at[8 - owner],
-            (dom, 2 * to + member),
-        )
-
-    edge_out = edge_send(member, outward, 0, 1)
-    edge_in = edge_send(1 - member, inward, 1, 1)
+    def step_sends(owner, to, k):
+        return [
+            copy(
+                source.at[1, at(HALO + owner * slab + ranked(owner, i))],
+                source.at[1, at((1 - owner) * (HALO + main) + in_halo(owner, i))],
+                step_send.at[k, i],
+                step_recv.at[1 - owner, i],
+                (dom, 2 * to + member),
+            )
+            for i in range(HALO)
+        ]
+
+    edge_out = step_sends(member, outward, 0)
+    edge_in = step_sends(1 - member, inward, 1)
     sum_sends = []
     result = None
     for section in range(STEPS):
@@ -438,34 +449,15 @@
             ends = jnp.concatenate([grids[2, slab - HALO : slab], grids[3, 0:HALO]], axis=0)
             spread(half_step * ends, [*range(HALO), *range(HALO + main, total)])
 
-            @pl.when(has_lower)
-            def _():
-                for c in range(chunks):
-                    arrived(halo_raw.at[0, span(c, edge_rows)], edge_recv_sem.at[0, c])
-
-            @pl.when(has_upper)
-            def _():
-                for c in range(chunks):
-                    arrived(halo_raw.at[1, span(c, edge_rows)], edge_recv_sem.at[1, c])
-
-            lax.fori_loop(0, HALO, begin_edges, 0)
-        else:
-
-            @pl.when(has_lower)
-            def _():
-                arrived(source.at[1, pl.ds(0, edge)], recv_sem.at[7])
-
-            @pl.when(has_upper)
-            def _():
-                arrived(source.at[1, pl.ds(edge + main * cells, edge)], recv_sem.at[8])
-
         outer_terms(section)
-        part = contract(ini[0], rounded[own_rows, :]) + contract(ini[1], turned[own_rows, :])
+        part = contract(own_turned[0], rounded[own_rows, :]) + contract(own_turned[1], turned[own_rows, :])
         if section == 0:
             arrived(other_ini, recv_sem.at[6])
             loads[3].wait()
-        part = part + contract(other_ini[0], rounded[other_rows, :])
-        part = part + contract(other_ini[1], turned[other_rows, :])
+            for half_index in range(2):
+                other_turned[half_index] = other_ini[half_index].T
+        part = part + contract(other_turned[0], rounded[other_rows, :])
+        part = part + contract(other_turned[1], turned[other_rows, :])
         sums[section, pair] = (part * (1.0 / cells_total)).astype(sums.dtype)
         for step in range(1, pairs):
             item = copy(
@@ -494,14 +486,16 @@
 
             @pl.when(has_outward)
             def _():
-                edge_out.start()
+                for item in edge_out:
+                    item.start()
 
         correction(section, other_ini, 1 - member, mixes)
         if section < STEPS - 1:
 
             @pl.when(has_inward)
             def _():
-                edge_in.start()
+                for item in edge_in:
+                    item.start()
 
     loads[4].wait()
     loads[5].wait()
@@ -605,11 +599,13 @@
 
     @pl.when(has_outward)
     def _():
-        edge_out.wait_send()
+        for item in edge_out:
+            item.wait_send()
 
     @pl.when(has_inward)
     def _():
-        edge_in.wait_send()
+        for item in edge_in:
+            item.wait_send()
         for item in [grid_forward] + raw_forward:
             item.wait_send()
 
@@ -672,10 +668,14 @@
             dma((STEPS, pairs)),
             dma((2 * doms,)),
             dma((2 * doms,)),
-            dma((2,)),
-            dma((2,)),
-            dma((2, 2)),
-            dma((2, 2)),
+            dma((slab,)),
+            dma((slab,)),
+            dma((2, HALO)),
+            dma((2, HALO)),
+            dma((2, HALO)),
+            dma((2, HALO)),
+            pltpu.VMEM((2, norb, rows), BF16),
+            pltpu.VMEM((2, norb, rows), BF16),
         ],
         compiler_params=pltpu.CompilerParams(
             collective_id=0, has_side_effects=True, vmem_limit_bytes=60 * 1024 * 1024

time: 43.9 us -> 43.7 us (level)
  no operation moved by 1% of the time
where the time goes in v4:
time: 43.7 us; the launch traced here: 43.5 us
  Pallas kernels  39.9 us (91%)
  local copies, waits for them, and re-layouts  2.95 us (7%)
  between operations  0.65 us (1%)
    pallas_call x1, Pallas kernels, shards(): pl.pallas_call(functools.partial(body, sizes), out_shape=(jax.ShapeDtypeS...  39.9 us
    unnamed x7, local copies, waits for them, and re-layouts  2.95 us

profile of v4, /device:TPU:0, one launch (start us, length us, event | category | flops | bytes accessed | tf_op | source)
XLA Modules:
  0.0 43.5 jit_solution(2721172899206225558)
XLA Ops:
  0.6 39.9 %shard_map.103 = (bf16[2,512,128]{2,1,0:T(8,128)(2,1)}, f32[2,128,128]{2,1,0:T(8,128)}, f32[4,128]{1,0:T(4,128)}) custom-call(bf16[2,512,128]{2,1,0:T(8,128)(2,1)} %bitcast.10, bf16[2,512,128]{2,1,0:T(8,128)(2,1)} %bitcast.11, f32[4,128]{1,0:T(4,128)} %bitcast.14, f32[4,128]{1,0:T(4,128)} %bitcast.15, f32[1,128]{1,0:T(1,128)} %bitcast.19, ...), custom_call_target="tpu_custom_call" | custom-call | tf_op jit(solution)/shard_map/pallas_call | solution.py:630
  40.5 0.0 copy-start
  40.5 1.7 %copy.14 = bf16[1,2,4,16,8,128]{5,4,3,2,1,0:T(8,128)(2,1)} copy(bf16[1,2,4,16,8,128]{5,4,3,2,1,0:T(8,128)(2,1)} %bitcast.12) | data formatting | bytes 524288
  42.2 0.0 copy-done
  42.2 0.0 copy-start.1
  42.2 0.7 %copy.15 = f32[1,2,128,128]{3,2,1,0:T(8,128)} copy(f32[1,2,128,128]{3,2,1,0:T(8,128)S(1)} %bitcast.13) | data formatting | bytes 262144
  42.9 0.0 copy-done.1
  42.9 0.6 %copy.16 = f32[1,4,128]{2,1,0:T(4,128)} copy(f32[1,4,128]{2,1,0:T(4,128)S(1)} %bitcast.16) | data formatting | bytes 4096
Async XLA Ops:
  40.5 1.7 %copy-start = (f32[2,128,128]{2,1,0:T(8,128)S(1)}, f32[2,128,128]{2,1,0:T(8,128)}, u32[]{:S(2)}) copy-start(f32[2,128,128]{2,1,0:T(8,128)} %get-tuple-element.7) | copy-start | bytes 393220
  42.2 0.7 %copy-start.1 = (f32[4,128]{1,0:T(4,128)S(1)}, f32[4,128]{1,0:T(4,128)}, u32[]{:S(2)}) copy-start(f32[4,128]{1,0:T(4,128)} %get-tuple-element.8) | copy-start | bytes 6148

commit v5 on v4

--- a/solution.py
+++ b/solution.py
@@ -72,6 +72,10 @@
     step_recv,
     own_turned,
     other_turned,
+    evolved_store,
+    inter_store,
+    pot_store,
+    store_sem,
 ):
     doms, space, slab, rows_y, cols_z, norb = sizes
     cells = rows_y * cols_z
@@ -280,7 +284,7 @@
             def _():
                 raw_forward[i].start()
 
-        if i == slab // 2:
+        if i == 0:
             ini_swap.start()
 
         begin(other_raw[at(plane), :], HALO + (1 - member) * slab + plane)
@@ -430,6 +434,13 @@
             for i in range(HALO)
         ]
 
+    def split(value, axis, order):
+        head = value.astype(BF16)
+        parts = [head, (value - head.astype(F32)).astype(BF16)]
+        return jnp.concatenate([parts[k] for k in order], axis=axis)
+
+    loads[3].wait()
+    coup_parts = split(coup[...], 1, (0, 1, 0))
     edge_out = step_sends(member, outward, 0)
     edge_in = step_sends(1 - member, inward, 1)
     sum_sends = []
@@ -453,7 +464,6 @@
         part = contract(own_turned[0], rounded[own_rows, :]) + contract(own_turned[1], turned[own_rows, :])
         if section == 0:
             arrived(other_ini, recv_sem.at[6])
-            loads[3].wait()
             for half_index in range(2):
                 other_turned[half_index] = other_ini[half_index].T
         part = part + contract(other_turned[0], rounded[other_rows, :])
@@ -475,12 +485,16 @@
         result = sums[section, 0].astype(F32)
         for slot in range(1, pairs):
             result = result + sums[section, slot].astype(F32)
-        mix = jnp.dot(
-            coup[...], result, precision=lax.Precision.HIGHEST, preferred_element_type=F32
-        )
+        mix = dot(coup_parts, split(result, 0, (0, 0, 1)))
         mix = mix.astype(BF16)
         mix_turned = (-sign[:norb] * swap(mix.astype(F32))).astype(BF16)
         mixes = jnp.concatenate([mix_turned, mix], axis=0)
+        if section == STEPS - 1:
+            inter[member] = result
+            inter_swap = copy(
+                inter.at[member], inter.at[member], send_sem.at[9], recv_sem.at[9], partner
+            )
+            inter_swap.start()
         correction(section, ini, member, mixes)
         if section < STEPS - 1:
 
@@ -525,11 +539,11 @@
             dens_sends.append(item)
     back = copy(rounded.at[other_rows], returned, send_sem.at[10], recv_sem.at[10], partner)
     back.start()
-    inter[member] = result
-    inter_swap = copy(
-        inter.at[member], inter.at[member], send_sem.at[9], recv_sem.at[9], partner
-    )
-    inter_swap.start()
+    arrived(inter.at[1 - member], recv_sem.at[9])
+    inter_store[0] = jnp.where(left[:norb], inter[0], swap(inter[1]))
+    inter_store[1] = jnp.where(left[:norb], swap(inter[0]), inter[1])
+    stores = [pltpu.make_async_copy(inter_store, inter_out, store_sem.at[0])]
+    stores[0].start()
     for step in range(doms):
         for k in range(2):
             if step == 0 and k == 0:
@@ -572,7 +586,9 @@
     blended = jnp.where(is_even, blended[:slab], blended[slab:])
     root = jnp.exp(jnp.log(blended + 1e-06) * (1.0 / 3.0))
     new_grid = ext[...] - xc_factor * root
-    pot_out[...] = new_grid
+    pot_store[...] = new_grid
+    stores.append(pltpu.make_async_copy(pot_store, pot_out, store_sem.at[1]))
+    stores[1].start()
     table = trig_table(half_step * new_grid)
     arrived(returned, recv_sem.at[10])
 
@@ -586,12 +602,18 @@
         one = jnp.where(is_even, other_half, own_half)
         re = jnp.where(left, zero, swap(one))
         im = jnp.where(left, swap(zero), one)
-        evolved_out[0, here, :] = (cos_v * re + sin_v * im).astype(BF16)
-        evolved_out[1, here, :] = (cos_v * im - sin_v * re).astype(BF16)
-    arrived(inter.at[1 - member], recv_sem.at[9])
-    inter_out[0] = jnp.where(left[:norb], inter[0], swap(inter[1]))
-    inter_out[1] = jnp.where(left[:norb], swap(inter[0]), inter[1])
-
+        evolved_store[0, here, :] = (cos_v * re + sin_v * im).astype(BF16)
+        evolved_store[1, here, :] = (cos_v * im - sin_v * re).astype(BF16)
+        for part in range(2):
+            item = pltpu.make_async_copy(
+                evolved_store.at[part, here],
+                evolved_out.at[part, here],
+                store_sem.at[2 + 2 * j + part],
+            )
+            item.start()
+            stores.append(item)
+    for item in stores:
+        item.wait()
     @pl.when(has_outward)
     def _():
         for item in [grid_edge] + raw_edge:
@@ -623,7 +645,6 @@
     total = main + 2 * HALO
     pairs = space // 2
     sizes = (doms, space, slab, rows_y, cols_z, norb)
-    vmem = pl.BlockSpec(memory_space=pltpu.VMEM)
     hbm = pl.BlockSpec(memory_space=pltpu.HBM)
     smem = pl.BlockSpec(memory_space=pltpu.SMEM)
     dma = pltpu.SemaphoreType.DMA
@@ -635,7 +656,7 @@
             jax.ShapeDtypeStruct((slab, cells), F32),
         ),
         in_specs=[hbm] * 6 + [smem] * 2,
-        out_specs=(vmem, vmem, vmem),
+        out_specs=(hbm, hbm, hbm),
         scratch_shapes=[
             pltpu.VMEM((2, rows, norb), BF16),
             pltpu.VMEM((2, rows, norb), BF16),
@@ -676,6 +697,10 @@
             dma((2, HALO)),
             pltpu.VMEM((2, norb, rows), BF16),
             pltpu.VMEM((2, norb, rows), BF16),
+            pltpu.VMEM((2, rows, norb), BF16),
+            pltpu.VMEM((2, norb, norb), F32),
+            pltpu.VMEM((slab, cells), F32),
+            dma((2 + 2 * slab,)),
         ],
         compiler_params=pltpu.CompilerParams(
             collective_id=0, has_side_effects=True, vmem_limit_bytes=60 * 1024 * 1024

time: 43.7 us -> 42.7 us (0.977)
  Pallas kernels: 39.9 us -> 38.9 us
    pallas_call x1, Pallas kernels: 39.9 us -> 38.9 us  [shards(): pl.pallas_call(functools.partial(body, sizes), out_shape=(jax.ShapeDtypeS...]
where the time goes in v5:
time: 42.7 us; the launch traced here: 42.5 us
  Pallas kernels  38.9 us (91%)
  local copies, waits for them, and re-layouts  2.95 us (7%)
  between operations  0.65 us (2%)
    pallas_call x1, Pallas kernels, shards(): pl.pallas_call(functools.partial(body, sizes), out_shape=(jax.ShapeDtypeS...  38.9 us
    unnamed x7, local copies, waits for them, and re-layouts  2.95 us

profile of v5, /device:TPU:0, one launch (start us, length us, event | category | flops | bytes accessed | tf_op | source)
XLA Modules:
  0.0 42.5 jit_solution(17822895426100307416)
XLA Ops:
  0.6 38.9 %shard_map.103 = (bf16[2,512,128]{2,1,0:T(8,128)(2,1)}, f32[2,128,128]{2,1,0:T(8,128)}, f32[4,128]{1,0:T(4,128)}) custom-call(bf16[2,512,128]{2,1,0:T(8,128)(2,1)} %bitcast.10, bf16[2,512,128]{2,1,0:T(8,128)(2,1)} %bitcast.11, f32[4,128]{1,0:T(4,128)} %bitcast.14, f32[4,128]{1,0:T(4,128)} %bitcast.15, f32[1,128]{1,0:T(1,128)} %bitcast.19, ...), custom_call_target="tpu_custom_call" | custom-call | tf_op jit(solution)/shard_map/pallas_call | solution.py:651
  39.5 0.0 copy-start
  39.5 1.7 %copy.14 = bf16[1,2,4,16,8,128]{5,4,3,2,1,0:T(8,128)(2,1)} copy(bf16[1,2,4,16,8,128]{5,4,3,2,1,0:T(8,128)(2,1)} %bitcast.12) | data formatting | bytes 524288
  41.2 0.0 copy-done
  41.2 0.0 copy-start.1
  41.2 0.7 %copy.15 = f32[1,2,128,128]{3,2,1,0:T(8,128)} copy(f32[1,2,128,128]{3,2,1,0:T(8,128)S(1)} %bitcast.13) | data formatting | bytes 262144
  41.9 0.0 copy-done.1
  41.9 0.6 %copy.16 = f32[1,4,128]{2,1,0:T(4,128)} copy(f32[1,4,128]{2,1,0:T(4,128)S(1)} %bitcast.16) | data formatting | bytes 4096
Async XLA Ops:
  39.5 1.7 %copy-start = (f32[2,128,128]{2,1,0:T(8,128)S(1)}, f32[2,128,128]{2,1,0:T(8,128)}, u32[]{:S(2)}) copy-start(f32[2,128,128]{2,1,0:T(8,128)} %get-tuple-element.7) | copy-start | bytes 393220
  41.2 0.7 %copy-start.1 = (f32[4,128]{1,0:T(4,128)S(1)}, f32[4,128]{1,0:T(4,128)}, u32[]{:S(2)}) copy-start(f32[4,128]{1,0:T(4,128)} %get-tuple-element.8) | copy-start | bytes 6148
